TPU v7x, 32 devices: a whole 2x2x4 slice. The times are simulated.
32 devices in a mesh: gx: 16 (over z, y, core), gy: 2 (over x).
Axes of the slice: x: 2, y: 2, z: 4, core: 2. Of those that a mesh axis runs over, the one named last changes fastest.
Arguments:
- velocity: float32 [128, 64, 256], P('gx', 'gy'), may hold values from 1.5 to 4.5
- density: float32 [128, 64, 256], P('gx', 'gy'), may hold values from 1.8 to 2.6
- adjoint_last: float32 [128, 64, 256], P('gx', 'gy'), may hold values from -6 to 6
- adjoint_now: float32 [128, 64, 256], P('gx', 'gy'), may hold values from -6 to 6
- forward_accel: bfloat16 [8, 128, 64, 256], P(None, 'gx', 'gy'), may hold values from -6 to 6
- residual_panels: bfloat16 [16384, 128], P(('gx', 'gy')), may hold values from -6 to 6
- owner_slab: int32 [16384, 1], P(('gx', 'gy')), may hold values from 0 to 15; in each aligned block of 512 rows (0 to 511, 512 to 1023, ...) at most 32 rows name the same one
- receiver_cell: int32 [16384], P(('gx', 'gy')), may hold values from 0 to 65535
- trace_offset: int32 [16384], P(('gx', 'gy')), may hold values from 0 to 31
Outputs:
- sensitivity: float32 [64, 128, 32], P('gx', 'gy')
- adjoint_final: float32 [128, 64, 256], P('gx', 'gy')
Inputs may be any that keep to these rules, and one draw needn't show every extreme that they name: `owner_slab`: the rows of one device name one slab at most 32 times, a bound that some block reaches. `receiver_cell`: numbered (x * 32 + y) * 256 + z within the owner's block.
All inputs are finite; a program needn't handle non-finite values.
Results may differ from a plain program's by a relative error of at most 0.0003.
Values may be sent and summed in bfloat16 or wider, within the bound.
No kernel may reach another device: no remote copies, remote signals or barrier semaphores. Data moves between devices by JAX's collectives and lax.ppermute only.
A program may use at most 64 MiB of HBM per device.

v0:
```python
import jax
import jax.numpy as jnp
from jax import lax
from jax.sharding import PartitionSpec as P


def padded_2(array, sides, width):
    for axis, dim in sides:
        devices, length = (lax.axis_size(axis), array.shape[dim])
        up = [(i, (i + 1) % devices) for i in range(devices - 1)]
        down = [(j, i) for i, j in up]
        last = lax.slice_in_dim(array, length - width, length, axis=dim)
        leading = lax.slice_in_dim(array, 0, width, axis=dim)
        before = lax.ppermute(last, axis, up)
        after = lax.ppermute(leading, axis, down)
        array = jnp.concatenate([before, array, after], axis=dim)
    return array


def resample(panels, offsets, step_count):
    panel_len = panels.shape[1]
    half_width = panel_len // step_count
    values = panels.astype(jnp.float32)
    clock = (jnp.arange(panel_len, dtype=jnp.int32)[None, :] + offsets[:, None]).astype(jnp.float32)
    columns = []
    for moment in range(step_count):
        weights = (
            jnp.maximum(0.0, 1.0 - jnp.abs(clock - half_width * (moment + 1)) / half_width) * 0.25
        )
        columns.append(jnp.sum(values * weights, axis=1))
    return jnp.stack(columns, axis=1)


def face_list(padded):
    return [
        padded[2:, 1:-1, 1:-1],
        padded[:-2, 1:-1, 1:-1],
        padded[1:-1, 2:, 1:-1],
        padded[1:-1, :-2, 1:-1],
        padded[1:-1, 1:-1, 2:],
        padded[1:-1, 1:-1, :-2],
    ]


def coarsen(kernel):
    size_a, size_b, size_c = kernel.shape
    blocks = kernel.reshape(size_a // 2, 2, size_b // 2, 2, size_c // 2, 2)
    return jnp.sum(blocks, axis=(1, 3, 5)) * 0.125


def wave_step(wave, wave_prev, couplings):
    padded = padded_2(wave, (("gx", 0), ("gy", 1)), 1)
    padded = jnp.pad(padded, ((0, 0), (0, 0), (1, 1)))
    nearby = face_list(padded)
    laplace = couplings[0] * (nearby[0] - wave)
    for index in range(1, 6):
        laplace = laplace + couplings[index] * (nearby[index] - wave)
    return 2.0 * wave - wave_prev + laplace


def shards(
    velocity,
    density,
    adjoint_last,
    adjoint_now,
    forward_accel,
    residual_panels,
    owner_slab,
    receiver_cell,
    trace_offset,
):
    slab_count = lax.axis_size("gx")
    sensors = residual_panels.shape[0]
    slot_count = sensors // 16
    step_count = forward_accel.shape[0]
    panel_len = residual_panels.shape[1]
    shift_span = 2 * panel_len // step_count
    owners = owner_slab[:, 0]
    onehot = (owners[:, None] == jnp.arange(slab_count, dtype=jnp.int32)[None, :]).astype(jnp.int32)
    order_rank = jnp.sum(jnp.cumsum(onehot, axis=0) * onehot, axis=1) - 1
    target = owners * slot_count + order_rank
    packed = (
        jnp.zeros((slab_count * slot_count, panel_len), jnp.bfloat16)
        .at[target]
        .set(residual_panels)
    )
    codes = (
        jnp.zeros((slab_count * slot_count,), jnp.int32)
        .at[target]
        .set(receiver_cell * shift_span + trace_offset)
    )
    arrived, arrived_codes = (
        lax.all_to_all(
            packed.reshape(slab_count, slot_count, panel_len),
            "gx",
            split_axis=0,
            concat_axis=0,
            tiled=True,
        ),
        lax.all_to_all(
            codes.reshape(slab_count, slot_count), "gx", split_axis=0, concat_axis=0, tiled=True
        ),
    )
    arrived_codes = arrived_codes.reshape(-1)
    cell_ids = arrived_codes // shift_span
    amplitudes = resample(arrived.reshape(-1, panel_len), arrived_codes % shift_span, step_count)
    square = 0.11 * velocity
    stiffness = square * square * density
    rho_pad = padded_2(density, (("gx", 0), ("gy", 1)), 1)
    rho_pad = jnp.pad(rho_pad, ((0, 0), (0, 0), (1, 1)))
    couplings = [stiffness * (2.0 / (density + nearby)) for nearby in face_list(rho_pad)]
    wave_prev = adjoint_last
    wave = adjoint_now
    accumulated = jnp.zeros(wave.shape, jnp.float32)
    for moment in range(step_count):
        wave_next = wave_step(wave, wave_prev, couplings)
        wave_next = (
            wave_next.reshape(-1).at[cell_ids].add(amplitudes[:, moment]).reshape(wave.shape)
        )
        accumulated = accumulated + wave_next * forward_accel[moment].astype(jnp.float32)
        wave_prev, wave = (wave, wave_next)
    kernel = -2.0 / velocity * accumulated
    coarse_block = jnp.transpose(coarsen(kernel), (0, 2, 1))
    sensitivity = lax.all_to_all(coarse_block, "gy", split_axis=1, concat_axis=2, tiled=True)
    return (sensitivity, wave)


def solution(mesh):
    in_specs = (
        P("gx", "gy", None),
        P("gx", "gy", None),
        P("gx", "gy", None),
        P("gx", "gy", None),
        P(None, "gx", "gy", None),
        P(("gx", "gy"), None),
        P(("gx", "gy"), None),
        P(("gx", "gy")),
        P(("gx", "gy")),
    )
    out_specs = (P("gx", "gy", None), P("gx", "gy", None))
    return jax.shard_map(shards, mesh=mesh, in_specs=in_specs, out_specs=out_specs, check_vma=False)
```

profile of v0, /device:TPU:26, one launch (start us, length us, event | category | flops | bytes accessed | tf_op | source)
XLA Modules:
  0.0 243.3 jit_solution(6511288479198124720)
XLA Ops:
  3.3 4.5 %collective-permute-start = (f32[1,32,256]{2,1,0:T(8,128)S(1)}, f32[1,32,256]{2,1,0:T(8,128)S(1)}, u32[]{:S(2)}, u32[]{:S(2)}) collective-permute-start(f32[1,32,256]{2,1,0:T(8,128)S(1)} %get-tuple-element.50), channel_id=1, source_target_pairs={{2,0},{4,2},{6,4},{8,6},{10,8},{12,10},{14,12},{16,14},{18,16},{20... | collective-permute-start | bytes 98312 | tf_op jit(solution)/shard_map/ppermute | solution.py:15
  15.3 5.2 %all-to-all-start = ((s32[16,1,32]{2,1,0:T(1,128)}), s32[16,1,32]{2,1,0:T(1,128)S(1)}, u32[]{:S(2)}, u32[]{:S(2)}) async-start(s32[16,1,32]{2,1,0:T(1,128)} %all_to_all.22), calls=%async_computation | async-start | bytes 16384 | tf_op jit(solution)/shard_map/all_to_all | solution.py:100
  23.3 4.4 %collective-permute-start.1 = (f32[1,32,256]{2,1,0:T(8,128)S(1)}, f32[1,32,256]{2,1,0:T(8,128)S(1)}, u32[]{:S(2)}, u32[]{:S(2)}) collective-permute-start(f32[1,32,256]{2,1,0:T(8,128)S(1)} %get-tuple-element.51), channel_id=1, source_target_pairs={{2,0},{4,2},{6,4},{8,6},{10,8},{12,10},{14,12},{16,14},{18,16},{20... | collective-permute-start | bytes 98312 | tf_op jit(solution)/shard_map/ppermute | solution.py:15
  27.7 2.7 %scatter_custom_fusion.1 = bf16[512,128]{1,0:T(8,128)(2,1)} fusion(s32[512]{0:T(512)S(1)} %bitcast.102, bf16[512,128]{1,0:T(8,128)(2,1)} %param.14, bf16[]{:T(256)} %constant.79.clone.1), kind=kCustom, calls=%fused_computation.263 | custom fusion | bytes 131584 | tf_op jit(solution)/shard_map/scatter | solution.py:85
  30.4 5.1 %all-to-all-start.1 = ((bf16[16,32,128]{2,1,0:T(8,128)(2,1)}), bf16[16,32,128]{2,1,0:T(8,128)(2,1)S(1)}, u32[]{:S(2)}, u32[]{:S(2)}) async-start(bf16[16,32,128]{2,1,0:T(8,128)(2,1)} %bitcast.6), calls=%async_computation.1 | async-start | bytes 262144 | tf_op jit(solution)/shard_map/all_to_all | solution.py:93
  42.6 4.5 %collective-permute-start.5 = (f32[10,1,256]{2,1,0:T(1,128)S(1)}, f32[10,1,256]{2,1,0:T(1,128)S(1)}, u32[]{:S(2)}, u32[]{:S(2)}) collective-permute-start(f32[10,1,256]{2,1,0:T(1,128)S(1)} %get-tuple-element.34), channel_id=1, source_target_pairs={{1,0},{3,2},{5,4},{7,6},{9,8},{11,10},{13,12},{15,14},{17,16},{19,... | collective-permute-start | bytes 30728 | tf_op jit(solution)/shard_map/ppermute | solution.py:15
  48.8 3.9 %collective-permute-done.7 = f32[10,1,256]{2,1,0:T(1,128)S(1)} collective-permute-done((f32[10,1,256]{2,1,0:T(1,128)S(1)}, f32[10,1,256]{2,1,0:T(1,128)S(1)}, u32[]{:S(2)}, u32[]{:S(2)}) %collective-permute-start.7) | collective-permute-done | bytes 10272 | tf_op jit(solution)/shard_map/ppermute | solution.py:14
  56.9 3.4 %scatter_fusion = f32[65536]{0:T(1024)S(1)} fusion(f32[65536]{0:T(1024)S(1)} %bitcast.69, s32[512]{0:T(512)S(1)} %bitcast.88, f32[512]{0:T(512)S(1)} %reshape.458), kind=kCustom, calls=%fused_computation.2 | custom fusion | flops 512 | bytes 8192 | tf_op jit(solution)/shard_map/scatter-add | solution.py:118
  62.4 4.5 %collective-permute-start.8 = (f32[1,32,256]{2,1,0:T(8,128)S(1)}, f32[1,32,256]{2,1,0:T(8,128)S(1)}, u32[]{:S(2)}, u32[]{:S(2)}) collective-permute-start(f32[1,32,256]{2,1,0:T(8,128)S(1)} %slice.568), channel_id=1, source_target_pairs={{2,0},{4,2},{6,4},{8,6},{10,8},{12,10},{14,12},{16,14},{18,16},{20... | collective-permute-start | bytes 98312 | tf_op jit(solution)/shard_map/ppermute | solution.py:15
  71.6 4.2 %collective-permute-done.11 = f32[10,1,256]{2,1,0:T(1,128)S(1)} collective-permute-done((f32[10,1,256]{2,1,0:T(1,128)S(1)}, f32[10,1,256]{2,1,0:T(1,128)S(1)}, u32[]{:S(2)}, u32[]{:S(2)}) %collective-permute-start.11) | collective-permute-done | bytes 10272 | tf_op jit(solution)/shard_map/ppermute | solution.py:14
  77.5 3.5 %scatter_fusion.1 = f32[65536]{0:T(1024)S(1)} fusion(f32[65536]{0:T(1024)S(1)} %bitcast.70, s32[512]{0:T(512)S(1)} %bitcast.89, f32[512]{0:T(512)S(1)} %reshape.466), kind=kCustom, calls=%fused_computation.3 | custom fusion | flops 512 | bytes 8192 | tf_op jit(solution)/shard_map/scatter-add | solution.py:118
  83.0 4.5 %collective-permute-start.12 = (f32[1,32,256]{2,1,0:T(8,128)S(1)}, f32[1,32,256]{2,1,0:T(8,128)S(1)}, u32[]{:S(2)}, u32[]{:S(2)}) collective-permute-start(f32[1,32,256]{2,1,0:T(8,128)S(1)} %slice.581), channel_id=1, source_target_pairs={{2,0},{4,2},{6,4},{8,6},{10,8},{12,10},{14,12},{16,14},{18,16},{20... | collective-permute-start | bytes 98312 | tf_op jit(solution)/shard_map/ppermute | solution.py:15
  92.2 4.2 %collective-permute-done.15 = f32[10,1,256]{2,1,0:T(1,128)S(1)} collective-permute-done((f32[10,1,256]{2,1,0:T(1,128)S(1)}, f32[10,1,256]{2,1,0:T(1,128)S(1)}, u32[]{:S(2)}, u32[]{:S(2)}) %collective-permute-start.15) | collective-permute-done | bytes 10272 | tf_op jit(solution)/shard_map/ppermute | solution.py:14
  97.2 3.6 %scatter_fusion.2 = f32[65536]{0:T(1024)S(1)} fusion(f32[65536]{0:T(1024)S(1)} %bitcast.71, s32[512]{0:T(512)S(1)} %bitcast.90, f32[512]{0:T(512)S(1)} %reshape.474), kind=kCustom, calls=%fused_computation.4 | custom fusion | flops 512 | bytes 8192 | tf_op jit(solution)/shard_map/scatter-add | solution.py:118
  102.9 4.5 %collective-permute-start.16 = (f32[1,32,256]{2,1,0:T(8,128)S(1)}, f32[1,32,256]{2,1,0:T(8,128)S(1)}, u32[]{:S(2)}, u32[]{:S(2)}) collective-permute-start(f32[1,32,256]{2,1,0:T(8,128)S(1)} %slice.594), channel_id=1, source_target_pairs={{2,0},{4,2},{6,4},{8,6},{10,8},{12,10},{14,12},{16,14},{18,16},{20... | collective-permute-start | bytes 98312 | tf_op jit(solution)/shard_map/ppermute | solution.py:15
  112.1 4.2 %collective-permute-done.19 = f32[10,1,256]{2,1,0:T(1,128)S(1)} collective-permute-done((f32[10,1,256]{2,1,0:T(1,128)S(1)}, f32[10,1,256]{2,1,0:T(1,128)S(1)}, u32[]{:S(2)}, u32[]{:S(2)}) %collective-permute-start.19) | collective-permute-done | bytes 10272 | tf_op jit(solution)/shard_map/ppermute | solution.py:14
  117.1 3.5 %scatter_fusion.3 = f32[65536]{0:T(1024)S(1)} fusion(f32[65536]{0:T(1024)S(1)} %bitcast.72, s32[512]{0:T(512)S(1)} %bitcast.91, f32[512]{0:T(512)S(1)} %reshape.482), kind=kCustom, calls=%fused_computation.5 | custom fusion | flops 512 | bytes 8192 | tf_op jit(solution)/shard_map/scatter-add | solution.py:118
  122.6 4.5 %collective-permute-start.20 = (f32[1,32,256]{2,1,0:T(8,128)S(1)}, f32[1,32,256]{2,1,0:T(8,128)S(1)}, u32[]{:S(2)}, u32[]{:S(2)}) collective-permute-start(f32[1,32,256]{2,1,0:T(8,128)S(1)} %slice.607), channel_id=1, source_target_pairs={{2,0},{4,2},{6,4},{8,6},{10,8},{12,10},{14,12},{16,14},{18,16},{20... | collective-permute-start | bytes 98312 | tf_op jit(solution)/shard_map/ppermute | solution.py:15
  131.8 4.2 %collective-permute-done.23 = f32[10,1,256]{2,1,0:T(1,128)S(1)} collective-permute-done((f32[10,1,256]{2,1,0:T(1,128)S(1)}, f32[10,1,256]{2,1,0:T(1,128)S(1)}, u32[]{:S(2)}, u32[]{:S(2)}) %collective-permute-start.23) | collective-permute-done | bytes 10272 | tf_op jit(solution)/shard_map/ppermute | solution.py:14
  136.7 3.5 %scatter_fusion.4 = f32[65536]{0:T(1024)S(1)} fusion(f32[65536]{0:T(1024)S(1)} %bitcast.73, s32[512]{0:T(512)S(1)} %bitcast.92, f32[512]{0:T(512)S(1)} %reshape.490), kind=kCustom, calls=%fused_computation.6 | custom fusion | flops 512 | bytes 8192 | tf_op jit(solution)/shard_map/scatter-add | solution.py:118
  142.3 4.5 %collective-permute-start.24 = (f32[1,32,256]{2,1,0:T(8,128)S(1)}, f32[1,32,256]{2,1,0:T(8,128)S(1)}, u32[]{:S(2)}, u32[]{:S(2)}) collective-permute-start(f32[1,32,256]{2,1,0:T(8,128)S(1)} %slice.620), channel_id=1, source_target_pairs={{2,0},{4,2},{6,4},{8,6},{10,8},{12,10},{14,12},{16,14},{18,16},{20... | collective-permute-start | bytes 98312 | tf_op jit(solution)/shard_map/ppermute | solution.py:15
  151.5 4.2 %collective-permute-done.27 = f32[10,1,256]{2,1,0:T(1,128)S(1)} collective-permute-done((f32[10,1,256]{2,1,0:T(1,128)S(1)}, f32[10,1,256]{2,1,0:T(1,128)S(1)}, u32[]{:S(2)}, u32[]{:S(2)}) %collective-permute-start.27) | collective-permute-done | bytes 10272 | tf_op jit(solution)/shard_map/ppermute | solution.py:14
  156.4 3.5 %scatter_fusion.5 = f32[65536]{0:T(1024)S(1)} fusion(f32[65536]{0:T(1024)S(1)} %bitcast.74, s32[512]{0:T(512)S(1)} %bitcast.93, f32[512]{0:T(512)S(1)} %reshape.498), kind=kCustom, calls=%fused_computation.7 | custom fusion | flops 512 | bytes 8192 | tf_op jit(solution)/shard_map/scatter-add | solution.py:118
  163.2 4.5 %collective-permute-start.28 = (f32[1,32,256]{2,1,0:T(8,128)}, f32[1,32,256]{2,1,0:T(8,128)S(1)}, u32[]{:S(2)}, u32[]{:S(2)}) collective-permute-start(f32[1,32,256]{2,1,0:T(8,128)} %slice.633), channel_id=1, source_target_pairs={{2,0},{4,2},{6,4},{8,6},{10,8},{12,10},{14,12},{16,14},{18,16},{20... | collective-permute-start | bytes 98312 | tf_op jit(solution)/shard_map/ppermute | solution.py:15
  174.5 3.2 %collective-permute-done.31 = f32[10,1,256]{2,1,0:T(1,128)} collective-permute-done((f32[10,1,256]{2,1,0:T(1,128)}, f32[10,1,256]{2,1,0:T(1,128)}, u32[]{:S(2)}, u32[]{:S(2)}) %collective-permute-start.31) | collective-permute-done | bytes 10272 | tf_op jit(solution)/shard_map/ppermute | solution.py:14
  179.9 3.6 %scatter_fusion.6 = f32[65536]{0:T(1024)S(1)} fusion(f32[65536]{0:T(1024)S(1)} %bitcast.75, s32[512]{0:T(512)S(1)} %bitcast.94, f32[512]{0:T(512)} %reshape.506), kind=kCustom, calls=%fused_computation.8 | custom fusion | flops 512 | bytes 8192 | tf_op jit(solution)/shard_map/scatter-add | solution.py:118
  187.5 4.5 %collective-permute-start.32 = (f32[1,32,256]{2,1,0:T(8,128)}, f32[1,32,256]{2,1,0:T(8,128)S(1)}, u32[]{:S(2)}, u32[]{:S(2)}) collective-permute-start(f32[1,32,256]{2,1,0:T(8,128)} %slice.646), channel_id=1, source_target_pairs={{2,0},{4,2},{6,4},{8,6},{10,8},{12,10},{14,12},{16,14},{18,16},{20... | collective-permute-start | bytes 98312 | tf_op jit(solution)/shard_map/ppermute | solution.py:15
  199.3 3.0 %collective-permute-done.35 = f32[10,1,256]{2,1,0:T(1,128)} collective-permute-done((f32[10,1,256]{2,1,0:T(1,128)}, f32[10,1,256]{2,1,0:T(1,128)}, u32[]{:S(2)}, u32[]{:S(2)}) %collective-permute-start.35) | collective-permute-done | bytes 10272 | tf_op jit(solution)/shard_map/ppermute | solution.py:14
  205.0 3.6 %scatter_fusion.7 = f32[65536]{0:T(1024)S(1)} fusion(f32[65536]{0:T(1024)S(1)} %bitcast.76, s32[512]{0:T(512)S(1)} %bitcast.95, f32[512]{0:T(512)} %reshape.514), kind=kCustom, calls=%fused_computation.9 | custom fusion | flops 512 | bytes 8192 | tf_op jit(solution)/shard_map/scatter-add | solution.py:118
  210.5 18.1 %reshape.429 = f32[4,2,16,2,128,2]{5,4,3,2,1,0:T(8,128)} reshape(f32[8,32,256]{2,1,0:T(8,128)S(1)} %fusion.154) | data formatting | bytes 524288 | tf_op jit(solution)/shard_map/reshape | solution.py:47
  228.6 7.0 %reduce_sum.123 = f32[4,16,128]{2,1,0:T(8,128)S(1)} reduce(f32[4,2,16,2,128,2]{5,4,3,2,1,0:T(8,128)} %reshape.429, f32[]{:T(128)} %constant.70.clone.1), dimensions={1,3,5}, to_apply=%region_21.22 | reduce | flops 57344 | bytes 294916 | tf_op jit(solution)/shard_map/reduce_sum | solution.py:48
  236.0 5.0 %all_to_all.32 = f32[2,1,4096]{2,1,0:T(1,128)S(1)} all-to-all(f32[2,1,4096]{2,1,0:T(1,128)S(1)} %reshape.532), channel_id=1, replica_groups=mesh['gx'=16,'gy'=2] {'gy'}, dimensions={0} | all-to-all | bytes 65536 | tf_op jit(solution)/shard_map/all_to_all | solution.py:124
  (184 shorter events, 94.0 us)
Async XLA Ops:
  1.4 35.4 %collective-permute-start.2 = (f32[1,32,256]{2,1,0:T(8,128)S(1)}, f32[1,32,256]{2,1,0:T(8,128)S(1)}, u32[]{:S(2)}, u32[]{:S(2)}) collective-permute-start(f32[1,32,256]{2,1,0:T(8,128)S(1)} %get-tuple-element.49), channel_id=1, source_target_pairs={{0,2},{2,4},{4,6},{6,8},{8,10},{10,12},{12,14},{14,16},{16,18},{18... | collective-permute-start | bytes 98312 | tf_op jit(solution)/shard_map/ppermute | solution.py:14
  3.3 34.5 %collective-permute-start = (f32[1,32,256]{2,1,0:T(8,128)S(1)}, f32[1,32,256]{2,1,0:T(8,128)S(1)}, u32[]{:S(2)}, u32[]{:S(2)}) collective-permute-start(f32[1,32,256]{2,1,0:T(8,128)S(1)} %get-tuple-element.50), channel_id=1, source_target_pairs={{2,0},{4,2},{6,4},{8,6},{10,8},{12,10},{14,12},{16,14},{18,16},{20... | collective-permute-start | bytes 98312 | tf_op jit(solution)/shard_map/ppermute | solution.py:15
  15.3 15.1 %all-to-all-start = ((s32[16,1,32]{2,1,0:T(1,128)}), s32[16,1,32]{2,1,0:T(1,128)S(1)}, u32[]{:S(2)}, u32[]{:S(2)}) async-start(s32[16,1,32]{2,1,0:T(1,128)} %all_to_all.22), calls=%async_computation | async-start | bytes 16384 | tf_op jit(solution)/shard_map/all_to_all | solution.py:100
  21.2 20.4 %collective-permute-start.3 = (f32[1,32,256]{2,1,0:T(8,128)S(1)}, f32[1,32,256]{2,1,0:T(8,128)S(1)}, u32[]{:S(2)}, u32[]{:S(2)}) collective-permute-start(f32[1,32,256]{2,1,0:T(8,128)S(1)} %get-tuple-element.52), channel_id=1, source_target_pairs={{0,2},{2,4},{4,6},{6,8},{8,10},{10,12},{12,14},{14,16},{16,18},{18... | collective-permute-start | bytes 98312 | tf_op jit(solution)/shard_map/ppermute | solution.py:14
  23.3 19.3 %collective-permute-start.1 = (f32[1,32,256]{2,1,0:T(8,128)S(1)}, f32[1,32,256]{2,1,0:T(8,128)S(1)}, u32[]{:S(2)}, u32[]{:S(2)}) collective-permute-start(f32[1,32,256]{2,1,0:T(8,128)S(1)} %get-tuple-element.51), channel_id=1, source_target_pairs={{2,0},{4,2},{6,4},{8,6},{10,8},{12,10},{14,12},{16,14},{18,16},{20... | collective-permute-start | bytes 98312 | tf_op jit(solution)/shard_map/ppermute | solution.py:15
  30.4 25.1 %all-to-all-start.1 = ((bf16[16,32,128]{2,1,0:T(8,128)(2,1)}), bf16[16,32,128]{2,1,0:T(8,128)(2,1)S(1)}, u32[]{:S(2)}, u32[]{:S(2)}) async-start(bf16[16,32,128]{2,1,0:T(8,128)(2,1)} %bitcast.6), calls=%async_computation.1 | async-start | bytes 262144 | tf_op jit(solution)/shard_map/all_to_all | solution.py:93
  37.9 10.6 %collective-permute-start.4 = (f32[10,1,256]{2,1,0:T(1,128)S(1)}, f32[10,1,256]{2,1,0:T(1,128)S(1)}, u32[]{:S(2)}, u32[]{:S(2)}) collective-permute-start(f32[10,1,256]{2,1,0:T(1,128)S(1)} %get-tuple-element.32), channel_id=1, source_target_pairs={{1,0},{3,2},{5,4},{7,6},{9,8},{11,10},{13,12},{15,14},{17,16},{19,... | collective-permute-start | bytes 30728 | tf_op jit(solution)/shard_map/ppermute | solution.py:15
  40.3 8.2 %collective-permute-start.6 = (f32[10,1,256]{2,1,0:T(1,128)S(1)}, f32[10,1,256]{2,1,0:T(1,128)S(1)}, u32[]{:S(2)}, u32[]{:S(2)}) collective-permute-start(f32[10,1,256]{2,1,0:T(1,128)S(1)} %get-tuple-element.31), channel_id=1, source_target_pairs={{0,1},{2,3},{4,5},{6,7},{8,9},{10,11},{12,13},{14,15},{16,17},{18,... | collective-permute-start | bytes 30728 | tf_op jit(solution)/shard_map/ppermute | solution.py:14
  42.6 6.2 %collective-permute-start.5 = (f32[10,1,256]{2,1,0:T(1,128)S(1)}, f32[10,1,256]{2,1,0:T(1,128)S(1)}, u32[]{:S(2)}, u32[]{:S(2)}) collective-permute-start(f32[10,1,256]{2,1,0:T(1,128)S(1)} %get-tuple-element.34), channel_id=1, source_target_pairs={{1,0},{3,2},{5,4},{7,6},{9,8},{11,10},{13,12},{15,14},{17,16},{19,... | collective-permute-start | bytes 30728 | tf_op jit(solution)/shard_map/ppermute | solution.py:15
  47.2 5.6 %collective-permute-start.7 = (f32[10,1,256]{2,1,0:T(1,128)S(1)}, f32[10,1,256]{2,1,0:T(1,128)S(1)}, u32[]{:S(2)}, u32[]{:S(2)}) collective-permute-start(f32[10,1,256]{2,1,0:T(1,128)S(1)} %get-tuple-element.33), channel_id=1, source_target_pairs={{0,1},{2,3},{4,5},{6,7},{8,9},{10,11},{12,13},{14,15},{16,17},{18,... | collective-permute-start | bytes 30728 | tf_op jit(solution)/shard_map/ppermute | solution.py:14
  60.4 6.6 %collective-permute-start.9 = (f32[1,32,256]{2,1,0:T(8,128)S(1)}, f32[1,32,256]{2,1,0:T(8,128)S(1)}, u32[]{:S(2)}, u32[]{:S(2)}) collective-permute-start(f32[1,32,256]{2,1,0:T(8,128)S(1)} %slice.571), channel_id=1, source_target_pairs={{0,2},{2,4},{4,6},{6,8},{8,10},{10,12},{12,14},{14,16},{16,18},{18... | collective-permute-start | bytes 98312 | tf_op jit(solution)/shard_map/ppermute | solution.py:14
  62.4 6.1 %collective-permute-start.8 = (f32[1,32,256]{2,1,0:T(8,128)S(1)}, f32[1,32,256]{2,1,0:T(8,128)S(1)}, u32[]{:S(2)}, u32[]{:S(2)}) collective-permute-start(f32[1,32,256]{2,1,0:T(8,128)S(1)} %slice.568), channel_id=1, source_target_pairs={{2,0},{4,2},{6,4},{8,6},{10,8},{12,10},{14,12},{16,14},{18,16},{20... | collective-permute-start | bytes 98312 | tf_op jit(solution)/shard_map/ppermute | solution.py:15
  70.2 5.6 %collective-permute-start.11 = (f32[10,1,256]{2,1,0:T(1,128)S(1)}, f32[10,1,256]{2,1,0:T(1,128)S(1)}, u32[]{:S(2)}, u32[]{:S(2)}) collective-permute-start(f32[10,1,256]{2,1,0:T(1,128)S(1)} %get-tuple-element.29), channel_id=1, source_target_pairs={{0,1},{2,3},{4,5},{6,7},{8,9},{10,11},{12,13},{14,15},{16,17},{18,... | collective-permute-start | bytes 30728 | tf_op jit(solution)/shard_map/ppermute | solution.py:14
  81.0 6.6 %collective-permute-start.13 = (f32[1,32,256]{2,1,0:T(8,128)S(1)}, f32[1,32,256]{2,1,0:T(8,128)S(1)}, u32[]{:S(2)}, u32[]{:S(2)}) collective-permute-start(f32[1,32,256]{2,1,0:T(8,128)S(1)} %slice.584), channel_id=1, source_target_pairs={{0,2},{2,4},{4,6},{6,8},{8,10},{10,12},{12,14},{14,16},{16,18},{18... | collective-permute-start | bytes 98312 | tf_op jit(solution)/shard_map/ppermute | solution.py:14
  83.0 6.1 %collective-permute-start.12 = (f32[1,32,256]{2,1,0:T(8,128)S(1)}, f32[1,32,256]{2,1,0:T(8,128)S(1)}, u32[]{:S(2)}, u32[]{:S(2)}) collective-permute-start(f32[1,32,256]{2,1,0:T(8,128)S(1)} %slice.581), channel_id=1, source_target_pairs={{2,0},{4,2},{6,4},{8,6},{10,8},{12,10},{14,12},{16,14},{18,16},{20... | collective-permute-start | bytes 98312 | tf_op jit(solution)/shard_map/ppermute | solution.py:15
  90.8 5.6 %collective-permute-start.15 = (f32[10,1,256]{2,1,0:T(1,128)S(1)}, f32[10,1,256]{2,1,0:T(1,128)S(1)}, u32[]{:S(2)}, u32[]{:S(2)}) collective-permute-start(f32[10,1,256]{2,1,0:T(1,128)S(1)} %get-tuple-element.27), channel_id=1, source_target_pairs={{0,1},{2,3},{4,5},{6,7},{8,9},{10,11},{12,13},{14,15},{16,17},{18,... | collective-permute-start | bytes 30728 | tf_op jit(solution)/shard_map/ppermute | solution.py:14
  100.9 6.6 %collective-permute-start.17 = (f32[1,32,256]{2,1,0:T(8,128)S(1)}, f32[1,32,256]{2,1,0:T(8,128)S(1)}, u32[]{:S(2)}, u32[]{:S(2)}) collective-permute-start(f32[1,32,256]{2,1,0:T(8,128)S(1)} %slice.597), channel_id=1, source_target_pairs={{0,2},{2,4},{4,6},{6,8},{8,10},{10,12},{12,14},{14,16},{16,18},{18... | collective-permute-start | bytes 98312 | tf_op jit(solution)/shard_map/ppermute | solution.py:14
  102.9 6.1 %collective-permute-start.16 = (f32[1,32,256]{2,1,0:T(8,128)S(1)}, f32[1,32,256]{2,1,0:T(8,128)S(1)}, u32[]{:S(2)}, u32[]{:S(2)}) collective-permute-start(f32[1,32,256]{2,1,0:T(8,128)S(1)} %slice.594), channel_id=1, source_target_pairs={{2,0},{4,2},{6,4},{8,6},{10,8},{12,10},{14,12},{16,14},{18,16},{20... | collective-permute-start | bytes 98312 | tf_op jit(solution)/shard_map/ppermute | solution.py:15
  110.7 5.6 %collective-permute-start.19 = (f32[10,1,256]{2,1,0:T(1,128)S(1)}, f32[10,1,256]{2,1,0:T(1,128)S(1)}, u32[]{:S(2)}, u32[]{:S(2)}) collective-permute-start(f32[10,1,256]{2,1,0:T(1,128)S(1)} %get-tuple-element.25), channel_id=1, source_target_pairs={{0,1},{2,3},{4,5},{6,7},{8,9},{10,11},{12,13},{14,15},{16,17},{18,... | collective-permute-start | bytes 30728 | tf_op jit(solution)/shard_map/ppermute | solution.py:14
  120.6 6.6 %collective-permute-start.21 = (f32[1,32,256]{2,1,0:T(8,128)S(1)}, f32[1,32,256]{2,1,0:T(8,128)S(1)}, u32[]{:S(2)}, u32[]{:S(2)}) collective-permute-start(f32[1,32,256]{2,1,0:T(8,128)S(1)} %slice.610), channel_id=1, source_target_pairs={{0,2},{2,4},{4,6},{6,8},{8,10},{10,12},{12,14},{14,16},{16,18},{18... | collective-permute-start | bytes 98312 | tf_op jit(solution)/shard_map/ppermute | solution.py:14
  122.6 6.1 %collective-permute-start.20 = (f32[1,32,256]{2,1,0:T(8,128)S(1)}, f32[1,32,256]{2,1,0:T(8,128)S(1)}, u32[]{:S(2)}, u32[]{:S(2)}) collective-permute-start(f32[1,32,256]{2,1,0:T(8,128)S(1)} %slice.607), channel_id=1, source_target_pairs={{2,0},{4,2},{6,4},{8,6},{10,8},{12,10},{14,12},{16,14},{18,16},{20... | collective-permute-start | bytes 98312 | tf_op jit(solution)/shard_map/ppermute | solution.py:15
  130.4 5.6 %collective-permute-start.23 = (f32[10,1,256]{2,1,0:T(1,128)S(1)}, f32[10,1,256]{2,1,0:T(1,128)S(1)}, u32[]{:S(2)}, u32[]{:S(2)}) collective-permute-start(f32[10,1,256]{2,1,0:T(1,128)S(1)} %get-tuple-element.23), channel_id=1, source_target_pairs={{0,1},{2,3},{4,5},{6,7},{8,9},{10,11},{12,13},{14,15},{16,17},{18,... | collective-permute-start | bytes 30728 | tf_op jit(solution)/shard_map/ppermute | solution.py:14
  140.2 6.6 %collective-permute-start.25 = (f32[1,32,256]{2,1,0:T(8,128)S(1)}, f32[1,32,256]{2,1,0:T(8,128)S(1)}, u32[]{:S(2)}, u32[]{:S(2)}) collective-permute-start(f32[1,32,256]{2,1,0:T(8,128)S(1)} %slice.623), channel_id=1, source_target_pairs={{0,2},{2,4},{4,6},{6,8},{8,10},{10,12},{12,14},{14,16},{16,18},{18... | collective-permute-start | bytes 98312 | tf_op jit(solution)/shard_map/ppermute | solution.py:14
  142.3 6.1 %collective-permute-start.24 = (f32[1,32,256]{2,1,0:T(8,128)S(1)}, f32[1,32,256]{2,1,0:T(8,128)S(1)}, u32[]{:S(2)}, u32[]{:S(2)}) collective-permute-start(f32[1,32,256]{2,1,0:T(8,128)S(1)} %slice.620), channel_id=1, source_target_pairs={{2,0},{4,2},{6,4},{8,6},{10,8},{12,10},{14,12},{16,14},{18,16},{20... | collective-permute-start | bytes 98312 | tf_op jit(solution)/shard_map/ppermute | solution.py:15
  150.1 5.6 %collective-permute-start.27 = (f32[10,1,256]{2,1,0:T(1,128)S(1)}, f32[10,1,256]{2,1,0:T(1,128)S(1)}, u32[]{:S(2)}, u32[]{:S(2)}) collective-permute-start(f32[10,1,256]{2,1,0:T(1,128)S(1)} %get-tuple-element.21), channel_id=1, source_target_pairs={{0,1},{2,3},{4,5},{6,7},{8,9},{10,11},{12,13},{14,15},{16,17},{18,... | collective-permute-start | bytes 30728 | tf_op jit(solution)/shard_map/ppermute | solution.py:14
  160.5 7.2 %collective-permute-start.29 = (f32[1,32,256]{2,1,0:T(8,128)}, f32[1,32,256]{2,1,0:T(8,128)S(1)}, u32[]{:S(2)}, u32[]{:S(2)}) collective-permute-start(f32[1,32,256]{2,1,0:T(8,128)} %slice.636), channel_id=1, source_target_pairs={{0,2},{2,4},{4,6},{6,8},{8,10},{10,12},{12,14},{14,16},{16,18},{18... | collective-permute-start | bytes 98312 | tf_op jit(solution)/shard_map/ppermute | solution.py:14
  163.2 6.4 %collective-permute-start.28 = (f32[1,32,256]{2,1,0:T(8,128)}, f32[1,32,256]{2,1,0:T(8,128)S(1)}, u32[]{:S(2)}, u32[]{:S(2)}) collective-permute-start(f32[1,32,256]{2,1,0:T(8,128)} %slice.633), channel_id=1, source_target_pairs={{2,0},{4,2},{6,4},{8,6},{10,8},{12,10},{14,12},{16,14},{18,16},{20... | collective-permute-start | bytes 98312 | tf_op jit(solution)/shard_map/ppermute | solution.py:15
  171.9 5.9 %collective-permute-start.31 = (f32[10,1,256]{2,1,0:T(1,128)}, f32[10,1,256]{2,1,0:T(1,128)}, u32[]{:S(2)}, u32[]{:S(2)}) collective-permute-start(f32[10,1,256]{2,1,0:T(1,128)} %get-tuple-element.19), channel_id=1, source_target_pairs={{0,1},{2,3},{4,5},{6,7},{8,9},{10,11},{12,13},{14,15},{16,17},{18,... | collective-permute-start | bytes 30728 | tf_op jit(solution)/shard_map/ppermute | solution.py:14
  184.2 7.8 %collective-permute-start.33 = (f32[1,32,256]{2,1,0:T(8,128)}, f32[1,32,256]{2,1,0:T(8,128)S(1)}, u32[]{:S(2)}, u32[]{:S(2)}) collective-permute-start(f32[1,32,256]{2,1,0:T(8,128)} %slice.649), channel_id=1, source_target_pairs={{0,2},{2,4},{4,6},{6,8},{8,10},{10,12},{12,14},{14,16},{16,18},{18... | collective-permute-start | bytes 98312 | tf_op jit(solution)/shard_map/ppermute | solution.py:14
  187.5 6.4 %collective-permute-start.32 = (f32[1,32,256]{2,1,0:T(8,128)}, f32[1,32,256]{2,1,0:T(8,128)S(1)}, u32[]{:S(2)}, u32[]{:S(2)}) collective-permute-start(f32[1,32,256]{2,1,0:T(8,128)} %slice.646), channel_id=1, source_target_pairs={{2,0},{4,2},{6,4},{8,6},{10,8},{12,10},{14,12},{16,14},{18,16},{20... | collective-permute-start | bytes 98312 | tf_op jit(solution)/shard_map/ppermute | solution.py:15
  194.5 4.8 %collective-permute-start.34 = (f32[10,1,256]{2,1,0:T(1,128)}, f32[10,1,256]{2,1,0:T(1,128)S(1)}, u32[]{:S(2)}, u32[]{:S(2)}) collective-permute-start(f32[10,1,256]{2,1,0:T(1,128)} %get-tuple-element.18), channel_id=1, source_target_pairs={{1,0},{3,2},{5,4},{7,6},{9,8},{11,10},{13,12},{15,14},{17,16},{19,... | collective-permute-start | bytes 30728 | tf_op jit(solution)/shard_map/ppermute | solution.py:15
  196.4 5.9 %collective-permute-start.35 = (f32[10,1,256]{2,1,0:T(1,128)}, f32[10,1,256]{2,1,0:T(1,128)}, u32[]{:S(2)}, u32[]{:S(2)}) collective-permute-start(f32[10,1,256]{2,1,0:T(1,128)} %get-tuple-element.17), channel_id=1, source_target_pairs={{0,1},{2,3},{4,5},{6,7},{8,9},{10,11},{12,13},{14,15},{16,17},{18,... | collective-permute-start | bytes 30728 | tf_op jit(solution)/shard_map/ppermute | solution.py:14
  (7 other events, 46.4 us)
where the time goes:
time: 247 us; the launch traced here: 243 us
  starting transfers between devices  98.9 us (40%)
  other arithmetic  55.3 us (22%)
  waiting for transfers between devices  41.5 us (17%)
  local copies, waits for them, and re-layouts  40.8 us (17%)
  blocking collectives  5.01 us (2%)
    ppermute x18, starting transfers between devices, padded_2(): after = lax.ppermute(leading, axis, down)  59.4 us
    ppermute x18, waiting for transfers between devices, padded_2(): before = lax.ppermute(last, axis, up)  31.1 us
    ppermute x18, starting transfers between devices, padded_2(): before = lax.ppermute(last, axis, up)  29.2 us
    scatter-add x8, other arithmetic, shards(): wave_next.reshape(-1).at[cell_ids].add(amplitudes[:, moment])  28.1 us
    reshape x1, local copies, waits for them, and re-layouts, coarsen(): blocks = kernel.reshape(size_a // 2, 2, size_b // 2, 2, size_c // 2, 2)  18.1 us
    ppermute x18, waiting for transfers between devices, padded_2(): after = lax.ppermute(leading, axis, down)  10.4 us
    add x8, other arithmetic, wave_step(): return 2.0 * wave - wave_prev + laplace  7.46 us
    reduce_sum x1, other arithmetic, coarsen(): return jnp.sum(blocks, axis=(1, 3, 5)) * 0.125  6.98 us
  transfers between devices with their start and end apart: 38, of which 15 were waited for; matrix products, arithmetic and copies ran while one was open for 10% of the time, Pallas kernels for 0%

commit v1 on v0

v1 whole, which is shorter than its diff:
```python
import functools

import jax
import jax.numpy as jnp
from jax import lax
from jax.experimental import pallas as pl
from jax.experimental.pallas import tpu as pltpu
from jax.sharding import PartitionSpec as P

F32, BF16, I32 = jnp.float32, jnp.bfloat16, jnp.int32
NEAR = 3
VMEM = pl.BlockSpec(memory_space=pltpu.VMEM)


def iota(shape, dim):
    return lax.broadcasted_iota(I32, shape, dim)


def dot_t(a, b):
    return lax.dot_general(a, b, (((1,), (1,)), ((), ())), preferred_element_type=F32)


def parts_of(x, count):
    parts = []
    for _ in range(count):
        part = x.astype(BF16)
        parts.append(part)
        x = x - part.astype(F32)
    return parts


def one_hot(flags):
    return jnp.where(flags, 1.0, 0.0).astype(BF16)


def y_sides(n_gy):
    return ("swap",) if n_gy == 2 else ("high", "low")


def send_row(side, j, cy, reach):
    if side == "swap":
        return (cy - reach) * (1 - j)
    return 0 if side == "high" else cy - reach


def side_source(side, j, n_gy, cy, reach):
    if side == "swap":
        return 1 - j, (cy - reach) * j, j >= 0
    if side == "high":
        return jnp.minimum(j + 1, n_gy - 1), 0, j + 1 < n_gy
    return jnp.maximum(j - 1, 0), cy - reach, j > 0


def pack_kernel(n_gx, n_gy, steps, slots, panels_ref, owner_ref, cell_ref, offset_ref, out_ref):
    sensors, length = panels_ref.shape
    half = length // steps
    span = 2 * half
    row, sample = iota((span * steps, length), 0), iota((span * steps, length), 1)
    clock = (sample + row // steps).astype(F32)
    centre = ((row % steps + 1) * half).astype(F32)
    weights = jnp.maximum(0.0, 1.0 - jnp.abs(clock - centre) * (1.0 / half)) * 0.25
    shifted = dot_t(weights.astype(BF16), panels_ref[...])
    offsets = offset_ref[...]
    amplitudes = jnp.zeros((steps, sensors), F32)
    for o in range(span):
        amplitudes = jnp.where(offsets == o, shifted[o * steps : (o + 1) * steps], amplitudes)
    owners = owner_ref[...]
    named = iota((n_gx, sensors), 0) == owners
    earlier = one_hot(iota((sensors, sensors), 0) <= iota((sensors, sensors), 1))
    counts = jnp.dot(one_hot(named), earlier, preferred_element_type=F32)
    rank = jnp.sum(jnp.where(named, counts, 0.0), axis=0, keepdims=True).astype(I32) - 1
    target = owners * slots + rank
    places = n_gx * slots
    moved = one_hot(iota((places, sensors), 0) == target)
    code = cell_ref[...] + 1
    line = iota((8, sensors), 0)
    code_rows = jnp.where(line == 0, code >> 8, jnp.where(line == 1, code & 255, 0))
    rows = parts_of(amplitudes, 3) + [code_rows.astype(F32).astype(BF16)]
    packed = [dot_t(part, moved) for part in rows]
    packed_amp = packed[0] + packed[1] + packed[2]
    packed_code = packed[3][0:1] * 256.0 + packed[3][1:2]
    blank = jnp.zeros((8, 128), F32)
    width = places + 128
    amp_pad = pltpu.roll(jnp.concatenate([packed_amp, blank], axis=1), slots, 1)
    code_pad = jnp.concatenate([jnp.broadcast_to(packed_code, (8, places)), blank], axis=1)
    code_pad = pltpu.roll(code_pad, slots, 1)
    line = iota((8, width), 0)
    lines = jnp.zeros((8, width), F32)
    for r in range(3):
        lines = jnp.where(line == r, pltpu.roll(code_pad, (3 - r) * slots, 1), lines)
    lane = iota((8, 128), 1)
    for g in range(n_gx):
        at = (g * slots) // 128 * 128
        turn = (256 - (g * slots) % 128) % 256
        if at + 256 <= width:
            amp_window, code_window = amp_pad[:, at : at + 256], lines[:, at : at + 256]
            if turn:
                amp_window, code_window = pltpu.roll(amp_window, turn, 1), pltpu.roll(code_window, turn, 1)
        else:
            amp_window, code_window = amp_pad[:, at : at + 128], lines[:, at : at + 128]
        tile = jnp.where(lane < 3 * slots, amp_window[:, :128], code_window[:, :128])
        for j in range(n_gy):
            out_ref[g, j] = tile


def plane_counts(cx):
    return (cx, cx, cx - 1, cx - 1)


def prep_kernel(n_gy, reach, now_ref, rho_ref, last_ref, vel_ref, odd_ref, even_ref, *side_refs):
    cx, cy, nz = now_ref.shape
    i, j = lax.axis_index("gx"), lax.axis_index("gy")
    parity = lax.rem(i, 2)
    fields = (now_ref, rho_ref, last_ref, vel_ref)
    for out_ref, right in ((odd_ref, parity), (even_ref, 1 - parity)):
        at = 0
        for ref, count in zip(fields, plane_counts(cx)):
            first = right if count < cx else 0
            out_ref[at : at + count] = ref[pl.ds(first, count)].astype(BF16)
            at += count
        near = (cx - NEAR) * right
        for ref in fields:
            x = ref[pl.ds(near, NEAR)]
            out_ref[at : at + NEAR] = (x - x.astype(BF16).astype(F32)).astype(BF16)
            at += NEAR
    for n, side in enumerate(y_sides(n_gy)):
        row = send_row(side, j, cy, reach)
        y_ref, corner_ref = side_refs[2 * n], side_refs[2 * n + 1]
        for f, ref in enumerate(fields):
            x = ref[:, pl.ds(pl.multiple_of(row, reach), reach), :]
            y_ref[f] = x
            corner_ref[f] = x.reshape(cx * reach, nz).astype(BF16)


def sim_kernel(n_gx, n_gy, steps, slots, reach, *refs):
    sides = y_sides(n_gy)
    now_ref, rho_ref, last_ref, vel_ref, forward_ref, arrived_ref, odd_ref, even_ref = refs[:8]
    side_refs = refs[8 : 8 + 3 * len(sides)]
    outs = refs[8 + 3 * len(sides) :]
    if n_gy == 2:
        final_ref, mine_ref, send_ref = outs[:3]
        scratch = outs[3:]
    else:
        final_ref, coarse_ref = outs[:2]
        scratch = outs[2:]
    (w_ref, prev_ref, r_ref, s_ref, c0, cxu, cxd, cyu, cyd, czu, czd, inject, acc_ref, flat_ref) = scratch
    cx, cy, nz = now_ref.shape
    rows = cy + reach * len(sides)
    i, j = lax.axis_index("gx"), lax.axis_index("gy")
    parity = lax.rem(i, 2)

    ext = (w_ref, r_ref, prev_ref, s_ref)
    for ref, out in zip((now_ref, rho_ref, last_ref, vel_ref), ext):
        out[cx : 2 * cx, 0:cy] = ref[...]
    for ref, left in ((odd_ref, 1 - parity), (even_ref, parity)):
        base = 2 * cx * (1 - left)
        at = 0
        for out, count in zip(ext, plane_counts(cx)):
            first = base + left if count < cx else base
            out[pl.ds(first, count), 0:cy] = ref[at : at + count].astype(F32)
            at += count
        near = base + (cx - NEAR) * left
        for out in ext:
            out[pl.ds(near, NEAR), 0:cy] += ref[at : at + NEAR].astype(F32)
            at += NEAR
    for n in range(len(sides)):
        own_side, even_side, odd_side = side_refs[3 * n : 3 * n + 3]
        at = cy + reach * n
        for f, out in enumerate(ext):
            out[cx : 2 * cx, at : at + reach] = own_side[f]
            out[pl.ds(2 * cx * (1 - parity), cx), at : at + reach] = even_side[f]
            corner = odd_side[f].astype(F32).reshape(cx, reach, nz)
            out[pl.ds(2 * cx * parity, cx), at : at + reach] = corner

    width = slots * n_gx
    per = 128 // slots
    lane = iota((8, 128), 1)

    def gathered(strip, slab):
        tiles, codes = [], []
        for g0 in range(0, n_gx, per):
            tile, code = jnp.zeros((8, 128), F32), jnp.zeros((8, 128), F32)
            for k in range(per):
                x = arrived_ref[g0 + k, strip]
                here = (lane >= k * slots) & (lane < (k + 1) * slots)
                turn = ((k - slab) * slots) % 128
                tile = jnp.where(here, pltpu.roll(x, turn, 1) if turn else x, tile)
                turn = ((k - 3) * slots) % 128
                code = jnp.where(here, pltpu.roll(x, turn, 1) if turn else x, code)
            tiles.append(tile)
            codes.append(code[slab : slab + 1])
        return jnp.concatenate(tiles, axis=1), jnp.concatenate(codes, axis=1).astype(I32) - 1

    depths = iota((nz, width), 0)
    for slab in range(3):
        layers = [(max(t + 1 - cx * slab, 0), min(3 * cx - 1 - t - cx * slab, cx)) for t in range(steps)]
        amps, codes = gathered(j, slab)
        depth = one_hot(depths == (codes & (nz - 1)))
        cells = one_hot(iota((cx * cy, width), 0) == (codes >> 8))
        hi, lo = parts_of(amps, 2)
        for t in range(steps):
            a, b = layers[t]
            if b <= a:
                continue
            block = cells[a * cy : b * cy]
            out = dot_t(block * hi[t : t + 1], depth) + dot_t(block * lo[t : t + 1], depth)
            inject[t, slab * cx + a : slab * cx + b, 0:cy] = out.reshape(b - a, cy, nz)
        for n, side in enumerate(sides):
            strip, row, there = side_source(side, j, n_gy, cy, reach)
            amps, codes = gathered(strip, slab)
            depth = one_hot(depths == (codes & (nz - 1)))
            place = codes >> 8
            y = (place & (cy - 1)) - row
            inside = (codes >= 0) & (y >= 0) & (y < reach) & there
            place = jnp.where(inside, (place // cy) * reach + y, -1)
            cells = one_hot(iota((cx * reach, width), 0) == place)
            hi, lo = parts_of(amps, 2)
            block = jnp.concatenate([cells * hi[t : t + 1] for t in range(steps)], axis=0)
            out = dot_t(block, depth)
            block = jnp.concatenate([cells * lo[t : t + 1] for t in range(steps)], axis=0)
            out = (out + dot_t(block, depth)).reshape(steps, cx, reach, nz)
            at = cy + reach * n
            for t in range(steps):
                inject[t, slab * cx : (slab + 1) * cx, at : at + reach] = out[t]

    row_at, lane_at = iota((rows, nz), 0), iota((rows, nz), 1)
    brk = cy + reach - 1 if n_gy > 2 else jnp.where(j == 0, rows - 1, cy - 1)
    before = jnp.where(brk == rows - 1, 0, brk + 1)
    top, bottom = row_at == brk, row_at == before
    deep, shallow = lane_at == nz - 1, lane_at == 0

    def over(x):
        return 2.0 / jnp.where(x > 0.0, x, 1.0)

    def couple(x, carry):
        rho = r_ref[x]
        vel = 0.11 * s_ref[x]
        stiff = vel * vel * rho
        alone = over(rho)
        hxu, hxd = over(rho + r_ref[x + 1]), over(rho + r_ref[x - 1])
        hyu = jnp.where(top, alone, over(rho + pltpu.roll(rho, rows - 1, 0)))
        hyd = jnp.where(bottom, alone, pltpu.roll(hyu, 1, 0))
        hzu = jnp.where(deep, alone, over(rho + pltpu.roll(rho, nz - 1, 1)))
        hzd = jnp.where(shallow, alone, pltpu.roll(hzu, 1, 1))
        c0[x] = 2.0 - stiff * (((hxu + hxd) + (hyu + hyd)) + (hzu + hzd))
        cxu[x], cxd[x] = stiff * hxu, stiff * hxd
        cyu[x] = jnp.where(top, 0.0, stiff * hyu)
        cyd[x] = jnp.where(bottom, 0.0, stiff * hyd)
        czu[x] = jnp.where(deep, 0.0, stiff * hzu)
        czd[x] = jnp.where(shallow, 0.0, stiff * hzd)
        return carry

    lax.fori_loop(1, 3 * cx - 1, couple, 0)

    wave, prev = w_ref, prev_ref
    for t in range(steps):

        def stencil(x, wave=wave, prev=prev, t=t):
            w = wave[x]
            u = c0[x] * w - prev[x] + inject[t, x]
            u = u + (cxu[x] * wave[x + 1] + cxd[x] * wave[x - 1])
            u = u + (cyu[x] * pltpu.roll(w, rows - 1, 0) + cyd[x] * pltpu.roll(w, 1, 0))
            return u + (czu[x] * pltpu.roll(w, nz - 1, 1) + czd[x] * pltpu.roll(w, 1, 1))

        def outer(x, carry, prev=prev, stencil=stencil):
            prev[x] = stencil(x)
            return carry

        def inner(x, carry, prev=prev, stencil=stencil, t=t):
            u = stencil(x)
            term = u[0:cy] * forward_ref[t, x - cx].astype(F32)
            acc_ref[x - cx] = term if t == 0 else acc_ref[x - cx] + term
            if t == steps - 1:
                final_ref[x - cx] = u[0:cy]
            else:
                prev[x] = u
            return carry

        lax.fori_loop(t + 1, cx, outer, 0)
        lax.fori_loop(cx, 2 * cx, inner, 0)
        lax.fori_loop(2 * cx, 3 * cx - 1 - t, outer, 0)
        wave, prev = prev, wave

    blocks = []
    for a in range(0, cx, 2):
        pair = (-2.0 / vel_ref[a]) * acc_ref[a] + (-2.0 / vel_ref[a + 1]) * acc_ref[a + 1]
        blocks.append(pair * 0.125)
    flat = jnp.concatenate(blocks, axis=0)
    half_z = one_hot(iota((nz // 2, nz), 1) // 2 == iota((nz // 2, nz), 0))
    flat = sum(dot_t(half_z, part) for part in parts_of(flat, 3)[::-1])
    count = cx // 2 * cy
    at = iota((count, count if n_gy == 2 else count // 2), 0)
    to = iota((count, count if n_gy == 2 else count // 2), 1)
    if n_gy == 2:
        goal = at // cy * cy + j * (cy // 2) + at % cy // 2
    else:
        goal = at // 2
    half_y = one_hot(to == goal)
    flat = sum(jnp.dot(part, half_y, preferred_element_type=F32) for part in parts_of(flat, 3)[::-1])
    if n_gy == 2:
        flat_ref[...] = flat
        half = nz // 4
        mine_ref[...] = flat_ref[pl.ds(pl.multiple_of(j * half, half), half)]
        send_ref[...] = flat_ref[pl.ds(pl.multiple_of((1 - j) * half, half), half)]
    else:
        coarse_ref[...] = flat


def call(kernel, out_shape, args, scratch=(), limit=60 << 20):
    return pl.pallas_call(
        kernel,
        out_shape=out_shape,
        in_specs=[VMEM] * len(args),
        out_specs=jax.tree.map(lambda _: VMEM, out_shape),
        scratch_shapes=scratch,
        compiler_params=pltpu.CompilerParams(vmem_limit_bytes=limit),
    )(*args)


def shards(
    n_gx,
    n_gy,
    velocity,
    density,
    adjoint_last,
    adjoint_now,
    forward_accel,
    residual_panels,
    owner_slab,
    receiver_cell,
    trace_offset,
):
    cx, cy, nz = velocity.shape
    steps = forward_accel.shape[0]
    reach = steps
    sensors = residual_panels.shape[0]
    slots = sensors // 16
    sides = y_sides(n_gy)
    shape = jax.ShapeDtypeStruct
    fields = (adjoint_now, density, adjoint_last, velocity)

    planes = sum(plane_counts(cx)) + 4 * NEAR
    prep_out = [shape((planes, cy, nz), BF16)] * 2
    for _ in sides:
        prep_out += [shape((4, cx, reach, nz), F32), shape((4, cx * reach, nz), BF16)]
    prep = call(functools.partial(prep_kernel, n_gy, reach), prep_out, fields)
    odd = [(a, a + 1) for a in range(1, n_gx - 1, 2)]
    odd = odd + [(b, a) for a, b in odd]
    even = [(a, a ^ 1) for a in range(n_gx)]
    odd_got = lax.ppermute(prep[0], "gx", odd)
    side_got = []
    for n, side in enumerate(sides):
        if side == "swap":
            over_y = [(0, 1), (1, 0)]
        elif side == "high":
            over_y = [(b + 1, b) for b in range(n_gy - 1)]
        else:
            over_y = [(b, b + 1) for b in range(n_gy - 1)]
        corner = [(a * n_gy + c, b * n_gy + d) for a, b in odd for c, d in over_y]
        own_side = lax.ppermute(prep[2 + 2 * n], "gy", over_y)
        odd_side = lax.ppermute(prep[3 + 2 * n], ("gx", "gy"), corner)
        side_got.append((own_side, odd_side))
    even_got = lax.ppermute(prep[1], "gx", even)

    packed = call(
        functools.partial(pack_kernel, n_gx, n_gy, steps, slots),
        shape((n_gx, n_gy, 8, 128), F32),
        (
            residual_panels,
            owner_slab.reshape(1, sensors),
            receiver_cell.reshape(1, sensors),
            trace_offset.reshape(1, sensors),
        ),
    )
    arrived = lax.all_to_all(
        packed.reshape(n_gx * n_gy, 8, 128), ("gx", "gy"), split_axis=0, concat_axis=0, tiled=True
    ).reshape(n_gx, n_gy, 8, 128)
    side_args = []
    for own_side, odd_side in side_got:
        side_args += [own_side, lax.ppermute(own_side, "gx", even), odd_side]

    rows = cy + reach * len(sides)
    block = pltpu.VMEM((3 * cx, rows, nz), F32)
    if n_gy == 2:
        outs = [shape((nz // 4, cx // 2 * cy), F32)] * 2
    else:
        outs = [shape((nz // 2, cx * cy // 4), F32)]
    got = call(
        functools.partial(sim_kernel, n_gx, n_gy, steps, slots, reach),
        [shape((cx, cy, nz), F32)] + outs,
        fields + (forward_accel, arrived, odd_got, even_got) + tuple(side_args),
        [block] * 11
        + [
            pltpu.VMEM((steps, 3 * cx, rows, nz), F32),
            pltpu.VMEM((cx, cy, nz), F32),
            pltpu.VMEM((nz // 2, cx // 2 * cy), F32),
        ],
    )
    if n_gy == 2:
        final, mine, send = got
        whole = mine + lax.ppermute(send, "gy", [(0, 1), (1, 0)])
        sensitivity = jnp.transpose(whole.reshape(nz // 4, cx // 2, cy), (1, 0, 2))
    else:
        final, coarse = got
        coarse = jnp.transpose(coarse.reshape(nz // 2, cx // 2, cy // 2), (1, 0, 2))
        sensitivity = lax.all_to_all(coarse, "gy", split_axis=1, concat_axis=2, tiled=True)
    return sensitivity, final


def solution(mesh):
    in_specs = (
        P("gx", "gy", None),
        P("gx", "gy", None),
        P("gx", "gy", None),
        P("gx", "gy", None),
        P(None, "gx", "gy", None),
        P(("gx", "gy"), None),
        P(("gx", "gy"), None),
        P(("gx", "gy")),
        P(("gx", "gy")),
    )
    out_specs = (P("gx", "gy", None), P("gx", "gy", None))
    body = functools.partial(shards, mesh.shape["gx"], mesh.shape["gy"])
    return jax.shard_map(body, mesh=mesh, in_specs=in_specs, out_specs=out_specs, check_vma=False)
```

time: 247 us -> 63.3 us (0.26)
  the two profiles are of different devices: /device:TPU:26 before, /device:TPU:0 now
where the time goes in v1:
time: 63.3 us; the launch traced here: 63 us
  Pallas kernels  28.4 us (45%)
  waiting for transfers between devices  18.7 us (30%)
  starting transfers between devices  12.5 us (20%)
  local copies, waits for them, and re-layouts  1.9 us (3%)
  other arithmetic  0.77 us (1%)
  between operations  0.72 us (1%)
    pallas_call x3, Pallas kernels, call(): pl.pallas_call(kernel, out_shape=out_shape, in_specs=[VMEM] * len(args),...  28.4 us
    all_to_all x1, waiting for transfers between devices, shards(): lax.all_to_all(packed.reshape(n_gx * n_gy, 8, 128), ('gx', 'gy'), split_a...  7.92 us
    ppermute x1, waiting for transfers between devices, shards(): own_side = lax.ppermute(prep[2 + 2 * n], 'gy', over_y)  7.01 us
    all_to_all x1, starting transfers between devices, shards(): lax.all_to_all(packed.reshape(n_gx * n_gy, 8, 128), ('gx', 'gy'), split_a...  4.93 us
    ppermute x1, starting transfers between devices, shards(): even_got = lax.ppermute(prep[1], 'gx', even)  4.35 us
    ppermute x1, waiting for transfers between devices, shards(): whole = mine + lax.ppermute(send, 'gy', [(0, 1), (1, 0)])  3.76 us
    ppermute x1, starting transfers between devices, shards(): own_side = lax.ppermute(prep[2 + 2 * n], 'gy', over_y)  1.49 us
  transfers between devices with their start and end apart: 7, of which 3 were waited for; matrix products, arithmetic and copies ran while one was open for 0% of the time, Pallas kernels for 4%

profile of v1, /device:TPU:0, one launch (start us, length us, event | category | flops | bytes accessed | tf_op | source)
XLA Modules:
  0.0 63.0 jit_solution(298929641909348378)
XLA Ops:
  0.6 2.5 %shard_map.105 = (bf16[42,32,256]{2,1,0:T(8,128)(2,1)}, bf16[42,32,256]{2,1,0:T(8,128)(2,1)}, f32[4,8,8,256]{3,2,1,0:T(8,128)}, bf16[4,64,256]{2,1,0:T(8,128)(2,1)}) custom-call(f32[8,32,256]{2,1,0:T(8,128)} %refs_0_.1, f32[8,32,256]{2,1,0:T(8,128)} %refs_1_.1, f32[8,32,256]{2,1,0:T(8,128)} %refs_2_.1, f32[8,32,256]{2,1,0:T(8,128)} %refs_3_.1), custom_call_target="tpu_custom_call" | custom-call | tf_op jit(solution)/shard_map/pallas_call | solution.py:310
  3.1 0.7 %collective-permute-start = (bf16[42,32,256]{2,1,0:T(8,128)(2,1)}, bf16[42,32,256]{2,1,0:T(8,128)(2,1)S(1)}, u32[]{:S(2)}, u32[]{:S(2)}) collective-permute-start(bf16[42,32,256]{2,1,0:T(8,128)(2,1)} %get-tuple-element.9), channel_id=1, source_target_pairs={{2,4},{6,8},{10,12},{14,16},{18,20},{22,24},{26,28},{4,2},{8,6},{1... | collective-permute-start | bytes 2064392 | tf_op jit(solution)/shard_map/ppermute | solution.py:350
  3.8 4.4 %collective-permute-start.1 = (bf16[42,32,256]{2,1,0:T(8,128)(2,1)}, bf16[42,32,256]{2,1,0:T(8,128)(2,1)S(1)}, u32[]{:S(2)}, u32[]{:S(2)}) collective-permute-start(bf16[42,32,256]{2,1,0:T(8,128)(2,1)} %get-tuple-element.10), channel_id=1, source_target_pairs={{0,2},{2,0},{4,6},{6,4},{8,10},{10,8},{12,14},{14,12},{16,18},{18,... | collective-permute-start | bytes 2064392 | tf_op jit(solution)/shard_map/ppermute | solution.py:363
  8.2 1.5 %collective-permute-start.2 = (f32[4,8,8,256]{3,2,1,0:T(8,128)}, f32[4,8,8,256]{3,2,1,0:T(8,128)S(1)}, u32[]{:S(2)}, u32[]{:S(2)}) collective-permute-start(f32[4,8,8,256]{3,2,1,0:T(8,128)} %get-tuple-element.11), channel_id=1, source_target_pairs={{0,1},{1,0},{2,3},{3,2},{4,5},{5,4},{6,7},{7,6},{8,9},{9,8},{10,11... | collective-permute-start | bytes 786440 | tf_op jit(solution)/shard_map/ppermute | solution.py:360
  9.7 7.0 %collective-permute-done.2.refs_8_ = f32[4,8,8,256]{3,2,1,0:T(8,128)S(1)} collective-permute-done((f32[4,8,8,256]{3,2,1,0:T(8,128)}, f32[4,8,8,256]{3,2,1,0:T(8,128)S(1)}, u32[]{:S(2)}, u32[]{:S(2)}) %collective-permute-start.2) | collective-permute-done | bytes 262176 | tf_op jit(solution)/shard_map/ppermute | solution.py:360
  16.7 0.0 copy-start.3
  16.7 0.0 collective-permute-start.3
  16.7 2.8 %shard_map.104 = f32[16,2,8,128]{3,2,1,0:T(8,128)} custom-call(bf16[512,128]{1,0:T(8,128)(2,1)} %panels_ref.1, s32[1,512]{1,0:T(1,128)} %bitcast.11, s32[1,512]{1,0:T(1,128)} %bitcast.12, s32[1,512]{1,0:T(1,128)} %bitcast.13), custom_call_target="tpu_custom_call" | custom-call | tf_op jit(solution)/shard_map/pallas_call | solution.py:310
  19.5 0.0 copy-start.6
  19.5 0.0 copy-done.3
  19.5 4.9 %all-to-all-start = ((f32[32,8,128]{2,1,0:T(8,128)}), f32[32,8,128]{2,1,0:T(8,128)S(1)}, u32[]{:S(2)}, u32[]{:S(2)}) async-start(f32[32,8,128]{2,1,0:T(8,128)} %bitcast.9), calls=%async_computation | async-start | bytes 262144 | tf_op jit(solution)/shard_map/all_to_all | solution.py:375
  24.4 0.0 copy-done.6
  24.4 0.7 %collective-permute-start.4 = (bf16[4,64,256]{2,1,0:T(8,128)(2,1)S(1)}, bf16[4,64,256]{2,1,0:T(8,128)(2,1)S(1)}, u32[]{:S(2)}, u32[]{:S(2)}) collective-permute-start(bf16[4,64,256]{2,1,0:T(8,128)(2,1)S(1)} %copy-done.6), channel_id=1, source_target_pairs={{2,5},{3,4},{6,9},{7,8},{10,13},{11,12},{14,17},{15,16},{18,21},{1... | collective-permute-start | bytes 393224 | tf_op jit(solution)/shard_map/ppermute | solution.py:361
  25.1 0.0 collective-permute-done.4.refs_10_
  25.1 0.0 copy-start.5
  25.1 7.9 %all-to-all-done = f32[32,8,128]{2,1,0:T(8,128)S(1)} async-done(((f32[32,8,128]{2,1,0:T(8,128)}), f32[32,8,128]{2,1,0:T(8,128)S(1)}, u32[]{:S(2)}, u32[]{:S(2)}) %all-to-all-start) | async-done | bytes 131104 | tf_op jit(solution)/shard_map/all_to_all | solution.py:375
  33.0 0.0 copy-start.2
  33.0 0.0 collective-permute-done.3.refs_9_
  33.0 0.0 collective-permute-done.refs_6_
  33.0 0.0 copy-start
  33.0 0.0 collective-permute-done.1.refs_7_
  33.1 0.0 copy-start.1
  33.1 0.0 copy-done.5
  33.1 0.6 copy-done.2
  33.7 0.1 copy-done.4
  33.8 0.3 copy-done
  34.0 0.2 copy-done.1
  34.2 23.1 %shard_map.106 = (f32[8,32,256]{2,1,0:T(8,128)}, f32[64,128]{1,0:T(8,128)}, f32[64,128]{1,0:T(8,128)}) custom-call(f32[8,32,256]{2,1,0:T(8,128)} %refs_0_.1, f32[8,32,256]{2,1,0:T(8,128)} %refs_1_.1, f32[8,32,256]{2,1,0:T(8,128)} %refs_2_.1, f32[8,32,256]{2,1,0:T(8,128)} %refs_3_.1, bf16[8,8,32,256]{3,2,1,0:T(8,128)(2,1)} %refs_4_.1, ...), custom_call_target="tpu_custom_call" | custom-call | tf_op jit(solution)/shard_map/pallas_call | solution.py:310
  57.4 0.4 collective-permute-start.5
  57.7 3.8 %collective-permute-done.5 = f32[64,128]{1,0:T(8,128)S(1)} collective-permute-done((f32[64,128]{1,0:T(8,128)}, f32[64,128]{1,0:T(8,128)S(1)}, u32[]{:S(2)}, u32[]{:S(2)}) %collective-permute-start.5) | collective-permute-done | bytes 32800 | tf_op jit(solution)/shard_map/ppermute | solution.py:401
  61.5 0.8 %add.3 = f32[64,128]{1,0:T(8,128)S(1)} add(f32[64,128]{1,0:T(8,128)} %get-tuple-element.13, f32[64,128]{1,0:T(8,128)S(1)} %collective-permute-done.5) | non-fusion elementwise | flops 8192 | bytes 98304 | tf_op jit(solution)/shard_map/add | solution.py:401
  62.3 0.7 %copy.12 = f32[64,128]{0,1:T(8,128)} copy(f32[64,128]{1,0:T(8,128)S(1)} %add.3) | data formatting | bytes 65536 | tf_op jit(solution)/shard_map/add | solution.py:401
  (1 shorter events, 0.0 us)
Async XLA Ops:
  3.1 29.9 %collective-permute-start = (bf16[42,32,256]{2,1,0:T(8,128)(2,1)}, bf16[42,32,256]{2,1,0:T(8,128)(2,1)S(1)}, u32[]{:S(2)}, u32[]{:S(2)}) collective-permute-start(bf16[42,32,256]{2,1,0:T(8,128)(2,1)} %get-tuple-element.9), channel_id=1, source_target_pairs={{2,4},{6,8},{10,12},{14,16},{18,20},{22,24},{26,28},{4,2},{8,6},{1... | collective-permute-start | bytes 2064392 | tf_op jit(solution)/shard_map/ppermute | solution.py:350
  3.8 29.2 %collective-permute-start.1 = (bf16[42,32,256]{2,1,0:T(8,128)(2,1)}, bf16[42,32,256]{2,1,0:T(8,128)(2,1)S(1)}, u32[]{:S(2)}, u32[]{:S(2)}) collective-permute-start(bf16[42,32,256]{2,1,0:T(8,128)(2,1)} %get-tuple-element.10), channel_id=1, source_target_pairs={{0,2},{2,0},{4,6},{6,4},{8,10},{10,8},{12,14},{14,12},{16,18},{18,... | collective-permute-start | bytes 2064392 | tf_op jit(solution)/shard_map/ppermute | solution.py:363
  8.2 8.5 %collective-permute-start.2 = (f32[4,8,8,256]{3,2,1,0:T(8,128)}, f32[4,8,8,256]{3,2,1,0:T(8,128)S(1)}, u32[]{:S(2)}, u32[]{:S(2)}) collective-permute-start(f32[4,8,8,256]{3,2,1,0:T(8,128)} %get-tuple-element.11), channel_id=1, source_target_pairs={{0,1},{1,0},{2,3},{3,2},{4,5},{5,4},{6,7},{7,6},{8,9},{9,8},{10,11... | collective-permute-start | bytes 786440 | tf_op jit(solution)/shard_map/ppermute | solution.py:360
  16.7 2.8 %copy-start.3 = (f32[4,8,8,256]{3,2,1,0:T(8,128)}, f32[4,8,8,256]{3,2,1,0:T(8,128)S(1)}, u32[]{:S(2)}) copy-start(f32[4,8,8,256]{3,2,1,0:T(8,128)S(1)} %collective-permute-done.2.refs_8_) | copy-start | bytes 786436
  16.7 16.4 %collective-permute-start.3 = (f32[4,8,8,256]{3,2,1,0:T(8,128)S(1)}, f32[4,8,8,256]{3,2,1,0:T(8,128)S(1)}, u32[]{:S(2)}, u32[]{:S(2)}) collective-permute-start(f32[4,8,8,256]{3,2,1,0:T(8,128)S(1)} %collective-permute-done.2.refs_8_), channel_id=1, source_target_pairs={{0,2},{2,0},{4,6},{6,4},{8,10},{10,8},{12,14},{14,12},{16,18},{18,... | collective-permute-start | bytes 786440 | tf_op jit(solution)/shard_map/ppermute | solution.py:380
  19.5 4.9 %copy-start.6 = (bf16[4,64,256]{2,1,0:T(8,128)(2,1)S(1)}, bf16[4,64,256]{2,1,0:T(8,128)(2,1)}, u32[]{:S(2)}) copy-start(bf16[4,64,256]{2,1,0:T(8,128)(2,1)} %get-tuple-element.12) | copy-start | bytes 393220
  19.5 13.6 %all-to-all-start = ((f32[32,8,128]{2,1,0:T(8,128)}), f32[32,8,128]{2,1,0:T(8,128)S(1)}, u32[]{:S(2)}, u32[]{:S(2)}) async-start(f32[32,8,128]{2,1,0:T(8,128)} %bitcast.9), calls=%async_computation | async-start | bytes 262144 | tf_op jit(solution)/shard_map/all_to_all | solution.py:375
  24.4 0.7 %collective-permute-start.4 = (bf16[4,64,256]{2,1,0:T(8,128)(2,1)S(1)}, bf16[4,64,256]{2,1,0:T(8,128)(2,1)S(1)}, u32[]{:S(2)}, u32[]{:S(2)}) collective-permute-start(bf16[4,64,256]{2,1,0:T(8,128)(2,1)S(1)} %copy-done.6), channel_id=1, source_target_pairs={{2,5},{3,4},{6,9},{7,8},{10,13},{11,12},{14,17},{15,16},{18,21},{1... | collective-permute-start | bytes 393224 | tf_op jit(solution)/shard_map/ppermute | solution.py:361
  25.1 8.0 %copy-start.5 = (bf16[4,64,256]{2,1,0:T(8,128)(2,1)}, bf16[4,64,256]{2,1,0:T(8,128)(2,1)S(1)}, u32[]{:S(2)}) copy-start(bf16[4,64,256]{2,1,0:T(8,128)(2,1)S(1)} %collective-permute-done.4.refs_10_) | copy-start | bytes 393220
  33.0 0.7 %copy-start.2 = (f32[32,8,128]{2,1,0:T(8,128)}, f32[32,8,128]{2,1,0:T(8,128)S(1)}, u32[]{:S(2)}) copy-start(f32[32,8,128]{2,1,0:T(8,128)S(1)} %all-to-all-done) | copy-start | bytes 393220
  33.0 0.7 %copy-start.4 = (f32[4,8,8,256]{3,2,1,0:T(8,128)}, f32[4,8,8,256]{3,2,1,0:T(8,128)S(1)}, u32[]{:S(2)}) copy-start(f32[4,8,8,256]{3,2,1,0:T(8,128)S(1)} %collective-permute-done.3.refs_9_) | copy-start | bytes 786436
  33.0 1.0 %copy-start = (bf16[42,32,256]{2,1,0:T(8,128)(2,1)}, bf16[42,32,256]{2,1,0:T(8,128)(2,1)S(1)}, u32[]{:S(2)}) copy-start(bf16[42,32,256]{2,1,0:T(8,128)(2,1)S(1)} %collective-permute-done.refs_6_) | copy-start | bytes 2064388
  33.1 1.2 %copy-start.1 = (bf16[42,32,256]{2,1,0:T(8,128)(2,1)}, bf16[42,32,256]{2,1,0:T(8,128)(2,1)S(1)}, u32[]{:S(2)}) copy-start(bf16[42,32,256]{2,1,0:T(8,128)(2,1)S(1)} %collective-permute-done.1.refs_7_) | copy-start | bytes 2064388
  57.4 4.1 %collective-permute-start.5 = (f32[64,128]{1,0:T(8,128)}, f32[64,128]{1,0:T(8,128)S(1)}, u32[]{:S(2)}, u32[]{:S(2)}) collective-permute-start(f32[64,128]{1,0:T(8,128)} %get-tuple-element.14), channel_id=1, source_target_pairs={{0,1},{1,0},{2,3},{3,2},{4,5},{5,4},{6,7},{7,6},{8,9},{9,8},{10,11... | collective-permute-start | bytes 98312 | tf_op jit(solution)/shard_map/ppermute | solution.py:401

commit v2 on v1

v2 whole, which is shorter than its diff:
```python
import functools

import jax
import jax.numpy as jnp
from jax import lax
from jax.experimental import pallas as pl
from jax.experimental.pallas import tpu as pltpu
from jax.sharding import PartitionSpec as P

F32, BF16, I32 = jnp.float32, jnp.bfloat16, jnp.int32
NEAR = 3
NEAR_CORNER = 4
VMEM = pl.BlockSpec(memory_space=pltpu.VMEM)
ANY = pl.BlockSpec(memory_space=pl.ANY)
HBM = pl.BlockSpec(memory_space=pltpu.HBM)


def iota(shape, dim):
    return lax.broadcasted_iota(I32, shape, dim)


def dot_t(a, b):
    return lax.dot_general(a, b, (((1,), (1,)), ((), ())), preferred_element_type=F32)


def parts_of(x, count):
    parts = []
    for _ in range(count):
        part = x.astype(BF16)
        parts.append(part)
        x = x - part.astype(F32)
    return parts


def one_hot(flags):
    return jnp.where(flags, 1.0, 0.0).astype(BF16)


def y_sides(n_gy):
    return ("swap",) if n_gy == 2 else ("high", "low")


def send_row(side, j, cy, reach):
    if side == "swap":
        return (cy - reach) * (1 - j)
    return 0 if side == "high" else cy - reach


def side_source(side, j, n_gy, cy, reach):
    if side == "swap":
        return 1 - j, (cy - reach) * j, j >= 0
    if side == "high":
        return jnp.minimum(j + 1, n_gy - 1), 0, j + 1 < n_gy
    return jnp.maximum(j - 1, 0), cy - reach, j > 0


def pack_kernel(n_gx, n_gy, steps, slots, panels_ref, owner_ref, cell_ref, offset_ref, out_ref):
    sensors, length = panels_ref.shape
    half = length // steps
    span = 2 * half
    row, sample = iota((span * steps, length), 0), iota((span * steps, length), 1)
    clock = (sample + row // steps).astype(F32)
    centre = ((row % steps + 1) * half).astype(F32)
    weights = jnp.maximum(0.0, 1.0 - jnp.abs(clock - centre) * (1.0 / half)) * 0.25
    shifted = dot_t(weights.astype(BF16), panels_ref[...])
    offsets = offset_ref[...]
    amplitudes = jnp.zeros((steps, sensors), F32)
    for o in range(span):
        amplitudes = jnp.where(offsets == o, shifted[o * steps : (o + 1) * steps], amplitudes)
    owners = owner_ref[...]
    named = iota((n_gx, sensors), 0) == owners
    earlier = one_hot(iota((sensors, sensors), 0) <= iota((sensors, sensors), 1))
    counts = jnp.dot(one_hot(named), earlier, preferred_element_type=F32)
    rank = jnp.sum(jnp.where(named, counts, 0.0), axis=0, keepdims=True).astype(I32) - 1
    target = owners * slots + rank
    places = n_gx * slots
    moved = one_hot(iota((places, sensors), 0) == target)
    code = cell_ref[...] + 1
    line = iota((8, sensors), 0)
    code_rows = jnp.where(line == 0, code >> 8, jnp.where(line == 1, code & 255, 0))
    rows = parts_of(amplitudes, 3) + [code_rows.astype(F32).astype(BF16)]
    packed = [dot_t(part, moved) for part in rows]
    packed_amp = packed[0] + packed[1] + packed[2]
    packed_code = packed[3][0:1] * 256.0 + packed[3][1:2]
    blank = jnp.zeros((8, 128), F32)
    width = places + 128
    amp_pad = pltpu.roll(jnp.concatenate([packed_amp, blank], axis=1), slots, 1)
    code_pad = jnp.concatenate([jnp.broadcast_to(packed_code, (8, places)), blank], axis=1)
    code_pad = pltpu.roll(code_pad, slots, 1)
    line = iota((8, width), 0)
    lines = jnp.zeros((8, width), F32)
    for r in range(3):
        lines = jnp.where(line == r, pltpu.roll(code_pad, (3 - r) * slots, 1), lines)
    lane = iota((8, 128), 1)
    for g in range(n_gx):
        at = (g * slots) // 128 * 128
        turn = (256 - (g * slots) % 128) % 256
        if at + 256 <= width:
            amp_window, code_window = amp_pad[:, at : at + 256], lines[:, at : at + 256]
            if turn:
                amp_window, code_window = pltpu.roll(amp_window, turn, 1), pltpu.roll(code_window, turn, 1)
        else:
            amp_window, code_window = amp_pad[:, at : at + 128], lines[:, at : at + 128]
        tile = jnp.where(lane < 3 * slots, amp_window[:, :128], code_window[:, :128])
        for j in range(n_gy):
            out_ref[g, j] = tile


def plane_counts(cx):
    return (cx, cx, cx - 1, cx - 1)


def prep_kernel(n_gy, reach, now_ref, rho_ref, last_ref, vel_ref, odd_ref, even_ref, *side_refs):
    cx, cy, nz = now_ref.shape
    i, j = lax.axis_index("gx"), lax.axis_index("gy")
    parity = lax.rem(i, 2)
    fields = (now_ref, rho_ref, last_ref, vel_ref)
    for out_ref, right in ((odd_ref, parity), (even_ref, 1 - parity)):
        at = 0
        for ref, count in zip(fields, plane_counts(cx)):
            first = right if count < cx else 0
            out_ref[at : at + count] = ref[pl.ds(first, count)].astype(BF16)
            at += count
        near = (cx - NEAR) * right
        for ref in fields:
            x = ref[pl.ds(near, NEAR)]
            out_ref[at : at + NEAR] = (x - x.astype(BF16).astype(F32)).astype(BF16)
            at += NEAR
    for n, side in enumerate(y_sides(n_gy)):
        row = send_row(side, j, cy, reach)
        y_ref, corner_ref = side_refs[3 * n], side_refs[3 * n + 1]
        for f, ref in enumerate(fields):
            x = ref[:, pl.ds(pl.multiple_of(row, reach), reach), :]
            y_ref[f] = x
            for out_ref, right in ((corner_ref, parity), (side_refs[3 * n + 2], 1 - parity)):
                out_ref[f, 0 : cx * reach] = x.reshape(cx * reach, nz).astype(BF16)
                z = ref[pl.ds((cx - NEAR_CORNER) * right, NEAR_CORNER), pl.ds(pl.multiple_of(row, reach), reach), :]
                z = (z - z.astype(BF16).astype(F32)).reshape(NEAR_CORNER * reach, nz)
                out_ref[f, cx * reach :] = z.astype(BF16)


def sim_kernel(n_gx, n_gy, steps, slots, reach, *refs):
    sides = y_sides(n_gy)
    fields, forward_in, arrived_in, odd_in, even_in = refs[:4], *refs[4:8]
    side_in = refs[8 : 8 + 3 * len(sides)]
    refs = refs[8 + 3 * len(sides) :]
    final_out = refs[0]
    coarse_refs, refs = (refs[1:3], refs[3:]) if n_gy == 2 else (refs[1:2], refs[2:])
    (w_ref, r_ref, prev_ref, v_ref, c0, cxu, cxd, cyu, cyd, czu, czd, inject, acc_ref), refs = refs[:13], refs[13:]
    forward_ref, arrived_ref, odd_ref, even_ref, *corner_refs, sem = refs
    cx, cy, nz = fields[0].shape
    half = nz // 2
    halves = range(2)
    rows = cy + reach * len(sides)
    pad = 8
    i, j = lax.axis_index("gx"), lax.axis_index("gy")
    parity = lax.rem(i, 2)
    if n_gy == 2:
        own, halo = pad + reach * j, (pad + cy * (1 - j),)
    else:
        own, halo = pad + reach, (pad + reach + cy, pad)
    own = pl.multiple_of(own, 8)
    halo = [pl.multiple_of(at, 8) for at in halo]
    own_rows = pl.ds(own, cy)
    ext = (w_ref, r_ref, prev_ref, v_ref)
    even_base, odd_base = 2 * cx * (1 - parity), 2 * cx * parity

    copies = []

    def fetch(src, dst):
        copy = pltpu.make_async_copy(src, dst, sem.at[len(copies)])
        copy.start()
        copies.append(copy)
        return copy

    got_sensors = fetch(arrived_in, arrived_ref)
    got_fields = []
    for field, out in zip(fields, ext):
        for h in halves:
            got_fields.append(fetch(field.at[:, :, half * h : half * (h + 1)], out.at[cx : 2 * cx, h, own_rows]))
    got_halos = [fetch(odd_in, odd_ref), fetch(even_in, even_ref)]
    for n in range(len(sides)):
        own_side, even_side, odd_side = side_in[3 * n : 3 * n + 3]
        for f, out in enumerate(ext):
            for h in halves:
                lanes = slice(half * h, half * (h + 1))
                at = pl.ds(halo[n], reach)
                got_fields.append(fetch(own_side.at[f, :, :, lanes], out.at[cx : 2 * cx, h, at]))
        got_halos.append(fetch(odd_side, corner_refs[2 * n]))
        got_halos.append(fetch(even_side, corner_refs[2 * n + 1]))
    got_forward = fetch(forward_in, forward_ref)

    blank = jnp.zeros((3 * cx, 2, pad, half), F32)
    for out in (w_ref, r_ref, prev_ref):
        out[:, :, 0:pad] = blank
        out[:, :, pad + rows : pad + rows + 8] = blank

    width = slots * n_gx
    per = 128 // slots
    lane = iota((8, 128), 1)

    def turned(x, turn):
        return pltpu.roll(x, turn % 128, 1) if turn % 128 else x

    def gathered(strip):
        tiles, codes = [[], [], []], []
        for g0 in range(0, n_gx, per):
            tile, code = [jnp.zeros((8, 128), F32)] * 3, jnp.zeros((8, 128), F32)
            for k in range(per):
                x = arrived_ref[g0 + k, strip]
                here = (lane >= k * slots) & (lane < (k + 1) * slots)
                for slab in range(3):
                    tile[slab] = jnp.where(here, turned(x, (k - slab) * slots), tile[slab])
                code = jnp.where(here, turned(x, (k - 3) * slots), code)
            for slab in range(3):
                tiles[slab].append(tile[slab])
            codes.append(code)
        codes = jnp.concatenate(codes, axis=1)
        return [jnp.concatenate(t, axis=1) for t in tiles], codes.astype(I32) - 1, jnp.transpose(codes).astype(I32) - 1

    def spread(cells_at, amps, column, spans):
        depth = one_hot(iota((width, nz), 1) == (column & (nz - 1)))
        hi, lo = parts_of(amps, 2)
        out = 0.0
        for part in (lo, hi):
            block = jnp.concatenate([cells_at[a:b] * part[t : t + 1] for t, a, b in spans], axis=0)
            out = out + jnp.dot(block, depth, preferred_element_type=F32)
        return out

    got_sensors.wait()
    strips = [(j, None)]
    for side in sides:
        strip, row, there = side_source(side, j, n_gy, cy, reach)
        strips.append((strip, (row, there)))
    for n, (strip, beside) in enumerate(strips):
        amps, codes, columns = gathered(strip)
        tall = cy if beside is None else reach
        at = pl.ds(own - pad if beside is None else halo[n - 1] - pad, tall)
        for slab in range(3):
            code = codes[slab : slab + 1]
            place = code >> 8
            if beside is not None:
                y = (place & (cy - 1)) - beside[0]
                inside = (code >= 0) & (y >= 0) & (y < reach) & beside[1]
                place = jnp.where(inside, (place // cy) * reach + y, -1)
            cells = one_hot(iota((cx * tall, width), 0) == place)
            layers = [(max(t + 1 - cx * slab, 0), min(3 * cx - 1 - t - cx * slab, cx)) for t in range(steps)]
            spans = [(t, a * tall, b * tall) for t, (a, b) in enumerate(layers) if a < b]
            out = spread(cells, amps[slab], columns[:, slab : slab + 1], spans)
            first = 0
            for t, a, b in spans:
                value = out[first : first + b - a].reshape((b - a) // tall, tall, nz)
                first += b - a
                xs = slice(slab * cx + a // tall, slab * cx + b // tall)
                for h in halves:
                    inject[t, xs, h, at] = value[:, :, half * h : half * (h + 1)]

    for copy in got_fields + got_halos:
        copy.wait()
    for ref, left in ((odd_ref, 1 - parity), (even_ref, parity)):
        base = 2 * cx * (1 - left)
        at = 0
        for out, count in zip(ext, plane_counts(cx)):
            first = base + left if count < cx else base
            for h in halves:
                lanes = slice(half * h, half * (h + 1))
                out[pl.ds(first, count), h, own_rows] = ref[at : at + count, :, lanes].astype(F32)
            at += count
        near = base + (cx - NEAR) * left
        for out in ext:
            for h in halves:
                lanes = slice(half * h, half * (h + 1))
                out[pl.ds(near, NEAR), h, own_rows] += ref[at : at + NEAR, :, lanes].astype(F32)
            at += NEAR
    for n in range(len(sides)):
        for f, out in enumerate(ext):
            for ref, left in ((corner_refs[2 * n], 1 - parity), (corner_refs[2 * n + 1], parity)):
                corner = ref[f].astype(F32).reshape(cx + NEAR_CORNER, reach, nz)
                base = 2 * cx * (1 - left)
                near = base + (cx - NEAR_CORNER) * left
                for h in halves:
                    lanes, at = slice(half * h, half * (h + 1)), pl.ds(halo[n], reach)
                    out[pl.ds(base, cx), h, at] = corner[:cx, :, lanes]
                    out[pl.ds(near, NEAR_CORNER), h, at] += corner[cx:, :, lanes]

    lane = iota((rows, half), 1)
    last, first = lane == half - 1, lane == 0
    mid, above, below = slice(pad, pad + rows), slice(pad + 1, pad + rows + 1), slice(pad - 1, pad + rows - 1)

    def shifted(x0, x1):
        u0, u1 = pltpu.roll(x0, half - 1, 1), pltpu.roll(x1, half - 1, 1)
        d0, d1 = pltpu.roll(x0, 1, 1), pltpu.roll(x1, 1, 1)
        return (jnp.where(last, u1, u0), u1), (d0, jnp.where(first, d0, d1))

    def over(x):
        return 2.0 / jnp.maximum(x, 1.0)

    def couple(x):
        rho = [r_ref[x, h, mid] for h in halves]
        deep, shallow = shifted(*rho)
        deep = (deep[0], jnp.where(last, 0.0, deep[1]))
        shallow = (jnp.where(first, 0.0, shallow[0]), shallow[1])
        for h in halves:
            vel = 0.11 * v_ref[x, h, mid]
            stiff = vel * vel * rho[h]
            xu, xd = stiff * over(rho[h] + r_ref[x + 1, h, mid]), stiff * over(rho[h] + r_ref[x - 1, h, mid])
            yu, yd = stiff * over(rho[h] + r_ref[x, h, above]), stiff * over(rho[h] + r_ref[x, h, below])
            zu, zd = stiff * over(rho[h] + deep[h]), stiff * over(rho[h] + shallow[h])
            c0[x, h] = 2.0 - (((xu + xd) + (yu + yd)) + (zu + zd))
            cxu[x, h], cxd[x, h], cyu[x, h], cyd[x, h] = xu, xd, yu, yd
            czu[x, h] = jnp.where(last, 0.0, zu) if h == 1 else zu
            czd[x, h] = jnp.where(first, 0.0, zd) if h == 0 else zd

    for x in range(1, 3 * cx - 1):
        couple(x)
    got_forward.wait()

    wave, prev = w_ref, prev_ref
    for t in range(steps):

        def advance(x, wave=wave, prev=prev, t=t):
            w = [wave[x, h, mid] for h in halves]
            deep, shallow = shifted(*w)
            for h in halves:
                u = c0[x, h] * w[h] - prev[x, h, mid] + inject[t, x, h]
                u = u + (cxu[x, h] * wave[x + 1, h, mid] + cxd[x, h] * wave[x - 1, h, mid])
                u = u + (cyu[x, h] * wave[x, h, above] + cyd[x, h] * wave[x, h, below])
                prev[x, h, mid] = u + (czu[x, h] * deep[h] + czd[x, h] * shallow[h])

        def gather(x, prev=prev, t=t):
            for h in halves:
                term = prev[cx + x, h, own_rows] * forward_ref[t, x, :, half * h : half * (h + 1)].astype(F32)
                acc_ref[x, h] = term if t == 0 else acc_ref[x, h] + term

        for x in range(t + 1, 3 * cx - 1 - t):
            advance(x)
            if cx <= x < 2 * cx:
                gather(x - cx)
        wave, prev = prev, wave
    out_copies = [
        fetch(wave.at[cx : 2 * cx, h, own_rows], final_out.at[:, :, half * h : half * (h + 1)]) for h in halves
    ]

    flat = []
    for h in halves:
        blocks = []
        for a in range(0, cx, 2):
            pair = sum((-0.25 / v_ref[cx + b, h, own_rows]) * acc_ref[b, h] for b in (a, a + 1))
            blocks.append(pair)
        flat.append(jnp.concatenate(blocks, axis=0))
    if n_gy == 2:
        flat = [jnp.where(j == h, flat[0], flat[1]) for h in halves]
    half_z = one_hot(iota((half, half // 2), 0) // 2 == iota((half, half // 2), 1))
    count = cx // 2 * cy
    tall = count if n_gy == 2 else count // 2
    to, at = iota((tall, count), 0), iota((tall, count), 1)
    goal = at // cy * cy + j * (cy // 2) + at % cy // 2 if n_gy == 2 else at // 2
    half_y = one_hot(to == goal)
    for h in halves:
        x = sum(jnp.dot(part, half_z, preferred_element_type=F32) for part in parts_of(flat[h], 3)[::-1])
        x = sum(jnp.dot(half_y, part, preferred_element_type=F32) for part in parts_of(x, 3)[::-1])
        if n_gy == 2:
            coarse_refs[h][...] = x.reshape(cx // 2, cy, half // 2)
        else:
            coarse_refs[0][:, half // 2 * h : half // 2 * (h + 1)] = x
    for copy in out_copies:
        copy.wait()


def call(kernel, out_shape, args, scratch=(), in_specs=None, out_specs=None, limit=60 << 20):
    return pl.pallas_call(
        kernel,
        out_shape=out_shape,
        in_specs=in_specs or [VMEM] * len(args),
        out_specs=out_specs or jax.tree.map(lambda _: VMEM, out_shape),
        scratch_shapes=scratch,
        compiler_params=pltpu.CompilerParams(vmem_limit_bytes=limit),
    )(*args)


def shards(
    n_gx,
    n_gy,
    velocity,
    density,
    adjoint_last,
    adjoint_now,
    forward_accel,
    residual_panels,
    owner_slab,
    receiver_cell,
    trace_offset,
):
    cx, cy, nz = velocity.shape
    steps = forward_accel.shape[0]
    reach = steps
    sensors = residual_panels.shape[0]
    slots = sensors // 16
    sides = y_sides(n_gy)
    shape = jax.ShapeDtypeStruct
    fields = (adjoint_now, density, adjoint_last, velocity)

    planes = sum(plane_counts(cx)) + 4 * NEAR
    prep_out = [shape((planes, cy, nz), BF16)] * 2
    for _ in sides:
        prep_out += [shape((4, cx, reach, nz), F32)] + [shape((4, (cx + NEAR_CORNER) * reach, nz), BF16)] * 2
    prep = call(functools.partial(prep_kernel, n_gy, reach), prep_out, fields)
    odd = [(a, a + 1) for a in range(1, n_gx - 1, 2)]
    odd = odd + [(b, a) for a, b in odd]
    even = [(a, a ^ 1) for a in range(n_gx)]
    packed = call(
        functools.partial(pack_kernel, n_gx, n_gy, steps, slots),
        shape((n_gx, n_gy, 8, 128), F32),
        (
            residual_panels,
            owner_slab.reshape(1, sensors),
            receiver_cell.reshape(1, sensors),
            trace_offset.reshape(1, sensors),
        ),
    )
    odd_got = lax.ppermute(prep[0], "gx", odd)
    side_got = []
    for n, side in enumerate(sides):
        if side == "swap":
            over_y = [(0, 1), (1, 0)]
        elif side == "high":
            over_y = [(b + 1, b) for b in range(n_gy - 1)]
        else:
            over_y = [(b, b + 1) for b in range(n_gy - 1)]
        corner = [(a * n_gy + c, b * n_gy + d) for a, b in odd for c, d in over_y]
        own_side = lax.ppermute(prep[2 + 3 * n], "gy", over_y)
        odd_side = lax.ppermute(prep[3 + 3 * n], ("gx", "gy"), corner)
        corner = [(a * n_gy + c, b * n_gy + d) for a, b in even for c, d in over_y]
        even_side = lax.ppermute(prep[4 + 3 * n], ("gx", "gy"), corner)
        side_got.append((own_side, even_side, odd_side))
    even_got = lax.ppermute(prep[1], "gx", even)

    arrived = lax.all_to_all(
        packed.reshape(n_gx * n_gy, 8, 128), ("gx", "gy"), split_axis=0, concat_axis=0, tiled=True
    ).reshape(n_gx, n_gy, 8, 128)
    side_args = [x for got in side_got for x in got]

    rows = cy + reach * len(sides)
    padded = pltpu.VMEM((3 * cx, 2, rows + 16, nz // 2), F32)
    block = pltpu.VMEM((3 * cx, 2, rows, nz // 2), F32)
    if n_gy == 2:
        outs = [shape((cx // 2, cy, nz // 4), F32)] * 2
    else:
        outs = [shape((cx * cy // 4, nz // 2), F32)]
    buffers = [forward_accel, arrived, odd_got, even_got] + [x for got in side_got for x in (got[2], got[1])]
    got = call(
        functools.partial(sim_kernel, n_gx, n_gy, steps, slots, reach),
        [shape((cx, cy, nz), F32)] + outs,
        fields + (forward_accel, arrived, odd_got, even_got) + tuple(side_args),
        [padded] * 4
        + [block] * 7
        + [pltpu.VMEM((steps, 3 * cx, 2, rows, nz // 2), F32), pltpu.VMEM((cx, 2, cy, nz // 2), F32)]
        + [pltpu.VMEM(x.shape, x.dtype) for x in buffers]
        + [pltpu.SemaphoreType.DMA((64,))],
        in_specs=[HBM] * 5 + [ANY] * (3 + len(side_args)),
        out_specs=[HBM] + [VMEM] * len(outs),
        limit=36 << 20,
    )
    if n_gy == 2:
        final, mine, send = got
        whole = mine + lax.ppermute(send, "gy", [(0, 1), (1, 0)])
        sensitivity = jnp.transpose(whole, (0, 2, 1))
    else:
        final, coarse = got
        coarse = jnp.transpose(coarse.reshape(cx // 2, cy // 2, nz // 2), (0, 2, 1))
        sensitivity = lax.all_to_all(coarse, "gy", split_axis=1, concat_axis=2, tiled=True)
    return sensitivity, final


def solution(mesh):
    in_specs = (
        P("gx", "gy", None),
        P("gx", "gy", None),
        P("gx", "gy", None),
        P("gx", "gy", None),
        P(None, "gx", "gy", None),
        P(("gx", "gy"), None),
        P(("gx", "gy"), None),
        P(("gx", "gy")),
        P(("gx", "gy")),
    )
    out_specs = (P("gx", "gy", None), P("gx", "gy", None))
    body = functools.partial(shards, mesh.shape["gx"], mesh.shape["gy"])
    return jax.shard_map(body, mesh=mesh, in_specs=in_specs, out_specs=out_specs, check_vma=False)
```

time: 63.3 us -> 47.1 us (0.74)
  the two profiles are of different devices: /device:TPU:0 before, /device:TPU:26 now
where the time goes in v2:
time: 47.1 us; the launch traced here: 46.9 us
  Pallas kernels  17.1 us (36%)
  starting transfers between devices  14.1 us (30%)
  waiting for transfers between devices  13 us (28%)
  local copies, waits for them, and re-layouts  1.24 us (3%)
  between operations  0.73 us (2%)
  other arithmetic  0.64 us (1%)
    pallas_call x3, Pallas kernels, call(): pl.pallas_call(kernel, out_shape=out_shape, in_specs=in_specs or [VMEM] *...  17.1 us
    all_to_all x1, starting transfers between devices, shards(): lax.all_to_all(packed.reshape(n_gx * n_gy, 8, 128), ('gx', 'gy'), split_a...  4.92 us
    ppermute x1, starting transfers between devices, shards(): odd_side = lax.ppermute(prep[3 + 3 * n], ('gx', 'gy'), corner)  4.21 us
    all_to_all x1, waiting for transfers between devices, shards(): lax.all_to_all(packed.reshape(n_gx * n_gy, 8, 128), ('gx', 'gy'), split_a...  4.2 us
    ppermute x1, waiting for transfers between devices, shards(): whole = mine + lax.ppermute(send, 'gy', [(0, 1), (1, 0)])  3.84 us
    ppermute x1, waiting for transfers between devices, shards(): even_side = lax.ppermute(prep[4 + 3 * n], ('gx', 'gy'), corner)  2.88 us
    ppermute x1, starting transfers between devices, shards(): odd_got = lax.ppermute(prep[0], 'gx', odd)  2.74 us
    ppermute x1, waiting for transfers between devices, shards(): odd_side = lax.ppermute(prep[3 + 3 * n], ('gx', 'gy'), corner)  2.05 us
  transfers between devices with their start and end apart: 7, of which 4 were waited for; matrix products, arithmetic and copies ran while one was open for 0% of the time, Pallas kernels for 6%

profile of v2, /device:TPU:26, one launch (start us, length us, event | category | flops | bytes accessed | tf_op | source)
XLA Modules:
  0.0 46.9 jit_solution(15707740167249464368)
XLA Ops:
  0.6 0.0 copy-start.2
  0.6 0.0 copy-start.3
  0.6 2.6 %shard_map.105 = (bf16[42,32,256]{2,1,0:T(8,128)(2,1)}, bf16[42,32,256]{2,1,0:T(8,128)(2,1)}, f32[4,8,8,256]{3,2,1,0:T(8,128)}, bf16[4,96,256]{2,1,0:T(8,128)(2,1)}, bf16[4,96,256]{2,1,0:T(8,128)(2,1)}) custom-call(f32[8,32,256]{2,1,0:T(8,128)} %refs_0_.1, f32[8,32,256]{2,1,0:T(8,128)} %refs_1_.1, f32[8,32,256]{2,1,0:T(8,128)} %refs_2_.1, f32[8,32,256]{2,1,0:T(8,128)} %refs_3_.1), custom_call_target="tpu_custom_call" | custom-call | tf_op jit(solution)/shard_map/pallas_call | solution.py:371
  3.3 2.7 %collective-permute-start = (bf16[42,32,256]{2,1,0:T(8,128)(2,1)}, bf16[42,32,256]{2,1,0:T(8,128)(2,1)S(1)}, u32[]{:S(2)}, u32[]{:S(2)}) collective-permute-start(bf16[42,32,256]{2,1,0:T(8,128)(2,1)} %get-tuple-element.10), channel_id=1, source_target_pairs={{2,4},{6,8},{10,12},{14,16},{18,20},{22,24},{26,28},{4,2},{8,6},{1... | collective-permute-start | bytes 2064392 | tf_op jit(solution)/shard_map/ppermute | solution.py:421
  6.0 0.9 %collective-permute-start.1 = (bf16[42,32,256]{2,1,0:T(8,128)(2,1)}, bf16[42,32,256]{2,1,0:T(8,128)(2,1)S(1)}, u32[]{:S(2)}, u32[]{:S(2)}) collective-permute-start(bf16[42,32,256]{2,1,0:T(8,128)(2,1)} %get-tuple-element.11), channel_id=1, source_target_pairs={{0,2},{2,0},{4,6},{6,4},{8,10},{10,8},{12,14},{14,12},{16,18},{18,... | collective-permute-start | bytes 2064392 | tf_op jit(solution)/shard_map/ppermute | solution.py:436
  6.9 0.5 %collective-permute-start.2 = (f32[4,8,8,256]{3,2,1,0:T(8,128)}, f32[4,8,8,256]{3,2,1,0:T(8,128)S(1)}, u32[]{:S(2)}, u32[]{:S(2)}) collective-permute-start(f32[4,8,8,256]{3,2,1,0:T(8,128)} %get-tuple-element.12), channel_id=1, source_target_pairs={{0,1},{1,0},{2,3},{3,2},{4,5},{5,4},{6,7},{7,6},{8,9},{9,8},{10,11... | collective-permute-start | bytes 786440 | tf_op jit(solution)/shard_map/ppermute | solution.py:431
  7.4 0.0 copy-start
  7.4 0.0 copy-start.1
  7.4 2.7 %shard_map.104 = f32[16,2,8,128]{3,2,1,0:T(8,128)} custom-call(bf16[512,128]{1,0:T(8,128)(2,1)} %panels_ref.1, s32[1,512]{1,0:T(1,128)} %bitcast.9, s32[1,512]{1,0:T(1,128)} %bitcast.10, s32[1,512]{1,0:T(1,128)} %bitcast.11), custom_call_target="tpu_custom_call" | custom-call | tf_op jit(solution)/shard_map/pallas_call | solution.py:371
  10.2 4.9 %all-to-all-start = ((f32[32,8,128]{2,1,0:T(8,128)}), f32[32,8,128]{2,1,0:T(8,128)S(1)}, u32[]{:S(2)}, u32[]{:S(2)}) async-start(f32[32,8,128]{2,1,0:T(8,128)} %bitcast.8), calls=%async_computation | async-start | bytes 262144 | tf_op jit(solution)/shard_map/all_to_all | solution.py:438
  15.1 0.4 collective-permute-start.3
  15.5 4.2 %collective-permute-start.4 = (bf16[4,96,256]{2,1,0:T(8,128)(2,1)}, bf16[4,96,256]{2,1,0:T(8,128)(2,1)S(1)}, u32[]{:S(2)}, u32[]{:S(2)}) collective-permute-start(bf16[4,96,256]{2,1,0:T(8,128)(2,1)} %get-tuple-element.14), channel_id=1, source_target_pairs={{2,5},{3,4},{6,9},{7,8},{10,13},{11,12},{14,17},{15,16},{18,21},{1... | collective-permute-start | bytes 589832 | tf_op jit(solution)/shard_map/ppermute | solution.py:432
  19.7 2.9 %collective-permute-done.3.refs_9_ = bf16[4,96,256]{2,1,0:T(8,128)(2,1)S(1)} collective-permute-done((bf16[4,96,256]{2,1,0:T(8,128)(2,1)}, bf16[4,96,256]{2,1,0:T(8,128)(2,1)S(1)}, u32[]{:S(2)}, u32[]{:S(2)}) %collective-permute-start.3) | collective-permute-done | bytes 196640 | tf_op jit(solution)/shard_map/ppermute | solution.py:434
  22.6 2.0 %collective-permute-done.4.refs_10_ = bf16[4,96,256]{2,1,0:T(8,128)(2,1)S(1)} collective-permute-done((bf16[4,96,256]{2,1,0:T(8,128)(2,1)}, bf16[4,96,256]{2,1,0:T(8,128)(2,1)S(1)}, u32[]{:S(2)}, u32[]{:S(2)}) %collective-permute-start.4) | collective-permute-done | bytes 196640 | tf_op jit(solution)/shard_map/ppermute | solution.py:432
  24.6 4.2 %all-to-all-done = f32[32,8,128]{2,1,0:T(8,128)S(1)} async-done(((f32[32,8,128]{2,1,0:T(8,128)}), f32[32,8,128]{2,1,0:T(8,128)S(1)}, u32[]{:S(2)}, u32[]{:S(2)}) %all-to-all-start) | async-done | bytes 131104 | tf_op jit(solution)/shard_map/all_to_all | solution.py:438
  28.8 0.0 collective-permute-done.2.refs_8_
  28.8 0.0 collective-permute-done.refs_6_
  28.8 0.0 collective-permute-done.1.refs_7_
  28.8 0.0 copy-done.2
  28.8 0.0 copy-done.3
  28.8 0.0 copy-done
  28.9 0.0 copy-done.1
  28.9 0.0 copy-start.4
  28.9 1.2 %copy-done.4 = bf16[8,8,32,256]{3,2,1,0:T(8,128)(2,1)S(1)} copy-done((bf16[8,8,32,256]{3,2,1,0:T(8,128)(2,1)S(1)}, bf16[8,8,32,256]{3,2,1,0:T(8,128)(2,1)}, u32[]{:S(2)}) %copy-start.4) | copy-done | bytes 1048600
  30.1 11.8 %shard_map.106 = (f32[8,32,256]{2,1,0:T(8,128)}, f32[4,32,64]{2,1,0:T(8,128)S(1)}, f32[4,32,64]{2,1,0:T(8,128)S(1)}) custom-call(f32[8,32,256]{2,1,0:T(8,128)S(1)} %copy-done, f32[8,32,256]{2,1,0:T(8,128)S(1)} %copy-done.1, f32[8,32,256]{2,1,0:T(8,128)S(1)} %copy-done.2, f32[8,32,256]{2,1,0:T(8,128)S(1)} %copy-done.3, bf16[8,8,32,256]{3,2,1,0:T(8,128)(2,1)S(1)} %copy-done.4, ...), custom_call_target="tpu_custom_call" | custom-call | tf_op jit(solution)/shard_map/pallas_call | solution.py:371
  41.9 0.5 %collective-permute-start.5 = (f32[4,32,64]{2,1,0:T(8,128)S(1)}, f32[4,32,64]{2,1,0:T(8,128)S(1)}, u32[]{:S(2)}, u32[]{:S(2)}) collective-permute-start(f32[4,32,64]{2,1,0:T(8,128)S(1)} %get-tuple-element.16), channel_id=1, source_target_pairs={{0,1},{1,0},{2,3},{3,2},{4,5},{5,4},{6,7},{7,6},{8,9},{9,8},{10,11... | collective-permute-start | bytes 98312 | tf_op jit(solution)/shard_map/ppermute | solution.py:466
  42.4 3.8 %collective-permute-done.5 = f32[4,32,64]{2,1,0:T(8,128)S(1)} collective-permute-done((f32[4,32,64]{2,1,0:T(8,128)S(1)}, f32[4,32,64]{2,1,0:T(8,128)S(1)}, u32[]{:S(2)}, u32[]{:S(2)}) %collective-permute-start.5) | collective-permute-done | bytes 32800 | tf_op jit(solution)/shard_map/ppermute | solution.py:466
  46.2 0.6 %add_bitcast_fusion = f32[4,64,32]{1,2,0:T(8,128)} fusion(f32[4,32,64]{2,1,0:T(8,128)S(1)} %get-tuple-element.15, f32[4,32,64]{2,1,0:T(8,128)S(1)} %collective-permute-done.5), kind=kLoop, calls=%fused_computation | loop fusion | flops 8192 | bytes 98304 | tf_op jit(solution)/shard_map/transpose | solution.py:467
Async XLA Ops:
  0.6 28.2 %copy-start.2 = (f32[8,32,256]{2,1,0:T(8,128)S(1)}, f32[8,32,256]{2,1,0:T(8,128)}, u32[]{:S(2)}) copy-start(f32[8,32,256]{2,1,0:T(8,128)} %refs_2_.1) | copy-start | bytes 786436
  0.6 28.2 %copy-start.3 = (f32[8,32,256]{2,1,0:T(8,128)S(1)}, f32[8,32,256]{2,1,0:T(8,128)}, u32[]{:S(2)}) copy-start(f32[8,32,256]{2,1,0:T(8,128)} %refs_3_.1) | copy-start | bytes 786436
  3.3 25.5 %collective-permute-start = (bf16[42,32,256]{2,1,0:T(8,128)(2,1)}, bf16[42,32,256]{2,1,0:T(8,128)(2,1)S(1)}, u32[]{:S(2)}, u32[]{:S(2)}) collective-permute-start(bf16[42,32,256]{2,1,0:T(8,128)(2,1)} %get-tuple-element.10), channel_id=1, source_target_pairs={{2,4},{6,8},{10,12},{14,16},{18,20},{22,24},{26,28},{4,2},{8,6},{1... | collective-permute-start | bytes 2064392 | tf_op jit(solution)/shard_map/ppermute | solution.py:421
  6.0 22.8 %collective-permute-start.1 = (bf16[42,32,256]{2,1,0:T(8,128)(2,1)}, bf16[42,32,256]{2,1,0:T(8,128)(2,1)S(1)}, u32[]{:S(2)}, u32[]{:S(2)}) collective-permute-start(bf16[42,32,256]{2,1,0:T(8,128)(2,1)} %get-tuple-element.11), channel_id=1, source_target_pairs={{0,2},{2,0},{4,6},{6,4},{8,10},{10,8},{12,14},{14,12},{16,18},{18,... | collective-permute-start | bytes 2064392 | tf_op jit(solution)/shard_map/ppermute | solution.py:436
  6.9 21.9 %collective-permute-start.2 = (f32[4,8,8,256]{3,2,1,0:T(8,128)}, f32[4,8,8,256]{3,2,1,0:T(8,128)S(1)}, u32[]{:S(2)}, u32[]{:S(2)}) collective-permute-start(f32[4,8,8,256]{3,2,1,0:T(8,128)} %get-tuple-element.12), channel_id=1, source_target_pairs={{0,1},{1,0},{2,3},{3,2},{4,5},{5,4},{6,7},{7,6},{8,9},{9,8},{10,11... | collective-permute-start | bytes 786440 | tf_op jit(solution)/shard_map/ppermute | solution.py:431
  7.4 21.4 %copy-start = (f32[8,32,256]{2,1,0:T(8,128)S(1)}, f32[8,32,256]{2,1,0:T(8,128)}, u32[]{:S(2)}) copy-start(f32[8,32,256]{2,1,0:T(8,128)} %refs_0_.1) | copy-start | bytes 786436
  7.4 21.4 %copy-start.1 = (f32[8,32,256]{2,1,0:T(8,128)S(1)}, f32[8,32,256]{2,1,0:T(8,128)}, u32[]{:S(2)}) copy-start(f32[8,32,256]{2,1,0:T(8,128)} %refs_1_.1) | copy-start | bytes 786436
  10.2 18.6 %all-to-all-start = ((f32[32,8,128]{2,1,0:T(8,128)}), f32[32,8,128]{2,1,0:T(8,128)S(1)}, u32[]{:S(2)}, u32[]{:S(2)}) async-start(f32[32,8,128]{2,1,0:T(8,128)} %bitcast.8), calls=%async_computation | async-start | bytes 262144 | tf_op jit(solution)/shard_map/all_to_all | solution.py:438
  15.1 7.5 %collective-permute-start.3 = (bf16[4,96,256]{2,1,0:T(8,128)(2,1)}, bf16[4,96,256]{2,1,0:T(8,128)(2,1)S(1)}, u32[]{:S(2)}, u32[]{:S(2)}) collective-permute-start(bf16[4,96,256]{2,1,0:T(8,128)(2,1)} %get-tuple-element.13), channel_id=1, source_target_pairs={{0,3},{1,2},{2,1},{3,0},{4,7},{5,6},{6,5},{7,4},{8,11},{9,10},{10,... | collective-permute-start | bytes 589832 | tf_op jit(solution)/shard_map/ppermute | solution.py:434
  15.5 9.1 %collective-permute-start.4 = (bf16[4,96,256]{2,1,0:T(8,128)(2,1)}, bf16[4,96,256]{2,1,0:T(8,128)(2,1)S(1)}, u32[]{:S(2)}, u32[]{:S(2)}) collective-permute-start(bf16[4,96,256]{2,1,0:T(8,128)(2,1)} %get-tuple-element.14), channel_id=1, source_target_pairs={{2,5},{3,4},{6,9},{7,8},{10,13},{11,12},{14,17},{15,16},{18,21},{1... | collective-permute-start | bytes 589832 | tf_op jit(solution)/shard_map/ppermute | solution.py:432
  28.9 1.2 %copy-start.4 = (bf16[8,8,32,256]{3,2,1,0:T(8,128)(2,1)S(1)}, bf16[8,8,32,256]{3,2,1,0:T(8,128)(2,1)}, u32[]{:S(2)}) copy-start(bf16[8,8,32,256]{3,2,1,0:T(8,128)(2,1)} %refs_4_.1) | copy-start | bytes 3145732
  41.9 4.3 %collective-permute-start.5 = (f32[4,32,64]{2,1,0:T(8,128)S(1)}, f32[4,32,64]{2,1,0:T(8,128)S(1)}, u32[]{:S(2)}, u32[]{:S(2)}) collective-permute-start(f32[4,32,64]{2,1,0:T(8,128)S(1)} %get-tuple-element.16), channel_id=1, source_target_pairs={{0,1},{1,0},{2,3},{3,2},{4,5},{5,4},{6,7},{7,6},{8,9},{9,8},{10,11... | collective-permute-start | bytes 98312 | tf_op jit(solution)/shard_map/ppermute | solution.py:466

commit v3 on v2

--- a/solution.py
+++ b/solution.py
@@ -9,7 +9,8 @@
 
 F32, BF16, I32 = jnp.float32, jnp.bfloat16, jnp.int32
 NEAR = 3
-NEAR_CORNER = 4
+NEAR_CORNER = 2
+HALF_ROWS = 4
 VMEM = pl.BlockSpec(memory_space=pltpu.VMEM)
 ANY = pl.BlockSpec(memory_space=pl.ANY)
 HBM = pl.BlockSpec(memory_space=pltpu.HBM)
@@ -110,33 +111,114 @@
     return (cx, cx, cx - 1, cx - 1)
 
 
-def prep_kernel(n_gy, reach, now_ref, rho_ref, last_ref, vel_ref, odd_ref, even_ref, *side_refs):
+def halo_planes(x_ref, out_ref, at, count, right):
+    cx = x_ref.shape[0]
+    first = right if count < cx else 0
+    out_ref[at : at + count] = x_ref[pl.ds(first, count)].astype(BF16)
+    x = x_ref[pl.ds((cx - NEAR) * right, NEAR)]
+    out_ref[at + count : at + count + NEAR] = (x - x.astype(BF16).astype(F32)).astype(BF16)
+
+
+def odd_kernel(*refs):
+    given, out, held, made, sem = refs[:4], refs[4], refs[5:9], refs[9], refs[10]
+    parity = lax.rem(lax.axis_index("gx"), 2)
+    copies = [pltpu.make_async_copy(src, dst, sem.at[n]) for n, (src, dst) in enumerate(zip(given, held))]
+    for copy in copies:
+        copy.start()
+    at, sent = 0, []
+    for n, count in enumerate(plane_counts(held[0].shape[0])):
+        copies[n].wait()
+        halo_planes(held[n], made, at, count, parity)
+        planes = pl.ds(at, count + NEAR)
+        sent.append(pltpu.make_async_copy(made.at[planes], out.at[planes], sem.at[4 + n]))
+        sent[-1].start()
+        at += count + NEAR
+    for copy in sent:
+        copy.wait()
+
+
+def second(x):
+    return x - x.astype(BF16).astype(F32)
+
+
+def fold(x, upper):
+    up = jnp.where(upper, 1, 0)
+    x = [x[n] for n in range(x.shape[0])]
+    turned = [pltpu.roll(y, HALF_ROWS, 0) for y in x]
+    row = iota(x[0].shape, 0)
+    pairs = []
+    for n in range(0, len(x), 2):
+        later = jnp.where(up == 1, x[n], turned[n])
+        sooner = jnp.where(up == 1, turned[n + 1], x[n + 1])
+        pairs.append(jnp.where(row < HALF_ROWS, sooner, later))
+    return pairs
+
+
+def unfold(pairs, upper):
+    up = jnp.where(upper, 1, 0)
+    layers = []
+    for y in pairs:
+        turned = pltpu.roll(y, HALF_ROWS, 0)
+        layers += [jnp.where(up == 1, y, turned), jnp.where(up == 1, turned, y)]
+    return layers
+
+
+def corner_tiles(cx):
+    return cx // 2 + (cx // 2 + NEAR_CORNER) // 2
+
+
+def tiles_of(x):
+    return [x[n : n + 8] for n in range(0, x.shape[0], 8)]
+
+
+def side_kernel(n_gy, reach, now_ref, rho_ref, last_ref, vel_ref, even_ref, *side_refs, done):
     cx, cy, nz = now_ref.shape
     i, j = lax.axis_index("gx"), lax.axis_index("gy")
     parity = lax.rem(i, 2)
     fields = (now_ref, rho_ref, last_ref, vel_ref)
-    for out_ref, right in ((odd_ref, parity), (even_ref, 1 - parity)):
-        at = 0
-        for ref, count in zip(fields, plane_counts(cx)):
-            first = right if count < cx else 0
-            out_ref[at : at + count] = ref[pl.ds(first, count)].astype(BF16)
-            at += count
-        near = (cx - NEAR) * right
-        for ref in fields:
-            x = ref[pl.ds(near, NEAR)]
-            out_ref[at : at + NEAR] = (x - x.astype(BF16).astype(F32)).astype(BF16)
-            at += NEAR
     for n, side in enumerate(y_sides(n_gy)):
         row = send_row(side, j, cy, reach)
-        y_ref, corner_ref = side_refs[3 * n], side_refs[3 * n + 1]
+        rows = pl.ds(pl.multiple_of(row, reach), reach)
+        y_ref, odd_ref, even_corner_ref = side_refs[3 * n : 3 * n + 3]
+        upper = row > 0
+        blocks = [[], []]
+        mid = cx // 2
         for f, ref in enumerate(fields):
-            x = ref[:, pl.ds(pl.multiple_of(row, reach), reach), :]
-            y_ref[f] = x
-            for out_ref, right in ((corner_ref, parity), (side_refs[3 * n + 2], 1 - parity)):
-                out_ref[f, 0 : cx * reach] = x.reshape(cx * reach, nz).astype(BF16)
-                z = ref[pl.ds((cx - NEAR_CORNER) * right, NEAR_CORNER), pl.ds(pl.multiple_of(row, reach), reach), :]
-                z = (z - z.astype(BF16).astype(F32)).reshape(NEAR_CORNER * reach, nz)
-                out_ref[f, cx * reach :] = z.astype(BF16)
+            y_ref[f] = ref[:, rows, :]
+            for block, right in ((blocks[0], parity), (blocks[1], 1 - parity)):
+                near = ref[pl.ds(mid * right, mid), rows, :]
+                block += [near[m] for m in range(mid)]
+                block += fold(ref[pl.ds(mid * (1 - right), mid), rows, :], upper)
+                block += fold(second(ref[pl.ds((cx - NEAR_CORNER) * right, NEAR_CORNER), rows, :]), upper)
+        for out_ref, block in zip((odd_ref, even_corner_ref), blocks):
+            out_ref[...] = jnp.concatenate(block, axis=0).astype(BF16)
+        for m in range(3):
+            done(1 + 3 * n + m)
+    at = 0
+    for ref, count in zip(fields, plane_counts(cx)):
+        halo_planes(ref, even_ref, at, count, 1 - parity)
+        at += count + NEAR
+    done(0)
+
+
+def stage_kernel(n_gx, n_gy, steps, slots, reach, *refs):
+    given, refs = refs[:8], refs[8:]
+    count = 2 + 3 * len(y_sides(n_gy))
+    outs, refs = refs[:count], refs[count:]
+    held, made, sem = refs[:8], refs[8 : 8 + count], refs[8 + count]
+    copies_in = [pltpu.make_async_copy(src, dst, sem.at[n]) for n, (src, dst) in enumerate(zip(given, held))]
+    copies_out = [pltpu.make_async_copy(src, dst, sem.at[8 + n]) for n, (src, dst) in enumerate(zip(made, outs))]
+    for copy in copies_in:
+        copy.start()
+    for copy in copies_in[:4]:
+        copy.wait()
+    pack_kernel(n_gx, n_gy, steps, slots, *held[:4], made[0])
+    copies_out[0].start()
+    for copy in copies_in[4:]:
+        copy.wait()
+    side_kernel(n_gy, reach, *held[4:], *made[1:], done=lambda n: copies_out[1 + n].start())
+    for copy in copies_out:
+        copy.wait()
 
 
 def sim_kernel(n_gx, n_gy, steps, slots, reach, *refs):
@@ -147,7 +229,7 @@
     final_out = refs[0]
     coarse_refs, refs = (refs[1:3], refs[3:]) if n_gy == 2 else (refs[1:2], refs[2:])
     (w_ref, r_ref, prev_ref, v_ref, c0, cxu, cxd, cyu, cyd, czu, czd, inject, acc_ref), refs = refs[:13], refs[13:]
-    forward_ref, arrived_ref, odd_ref, even_ref, *corner_refs, sem = refs
+    forward_ref, arrived_ref, odd_ref, even_ref, *side_refs, sem = refs
     cx, cy, nz = fields[0].shape
     half = nz // 2
     halves = range(2)
@@ -183,11 +265,10 @@
         own_side, even_side, odd_side = side_in[3 * n : 3 * n + 3]
         for f, out in enumerate(ext):
             for h in halves:
-                lanes = slice(half * h, half * (h + 1))
-                at = pl.ds(halo[n], reach)
-                got_fields.append(fetch(own_side.at[f, :, :, lanes], out.at[cx : 2 * cx, h, at]))
-        got_halos.append(fetch(odd_side, corner_refs[2 * n]))
-        got_halos.append(fetch(even_side, corner_refs[2 * n + 1]))
+                src = own_side.at[f, :, :, half * h : half * (h + 1)]
+                got_fields.append(fetch(src, out.at[cx : 2 * cx, h, pl.ds(halo[n], reach)]))
+        got_halos.append(fetch(odd_side, side_refs[2 * n]))
+        got_halos.append(fetch(even_side, side_refs[2 * n + 1]))
     got_forward = fetch(forward_in, forward_ref)
 
     blank = jnp.zeros((3 * cx, 2, pad, half), F32)
@@ -226,6 +307,47 @@
             block = jnp.concatenate([cells_at[a:b] * part[t : t + 1] for t, a, b in spans], axis=0)
             out = out + jnp.dot(block, depth, preferred_element_type=F32)
         return out
+
+    for copy in got_fields + got_halos:
+        copy.wait()
+    for ref, left in ((odd_ref, 1 - parity), (even_ref, parity)):
+        base = 2 * cx * (1 - left)
+        at = 0
+        near = base + (cx - NEAR) * left
+        for out, count in zip(ext, plane_counts(cx)):
+            first = base + left if count < cx else base
+            for h in halves:
+                lanes = slice(half * h, half * (h + 1))
+                out[pl.ds(first, count), h, own_rows] = ref[at : at + count, :, lanes].astype(F32)
+                out[pl.ds(near, NEAR), h, own_rows] += ref[at + count : at + count + NEAR, :, lanes].astype(F32)
+            at += count + NEAR
+    for n in range(len(sides)):
+        upper = side_source(sides[n], j, n_gy, cy, reach)[1] > 0
+        at = pl.ds(halo[n], reach)
+        mid = cx // 2
+
+        def put(out, x, tile, add=False):
+            for h in halves:
+                value = tile[:, half * h : half * (h + 1)]
+                if add:
+                    value = value + out[x, h, at]
+                out[x, h, at] = value
+
+        tall = corner_tiles(cx)
+        for ref, left in ((side_refs[2 * n], 1 - parity), (side_refs[2 * n + 1], parity)):
+            found = tiles_of(ref[...].astype(F32))
+            base = 2 * cx * (1 - left)
+            for f, out in enumerate(ext):
+                tiles = found[f * tall : (f + 1) * tall]
+                far = unfold(tiles[mid : mid + mid // 2], upper)
+                more = unfold(tiles[mid + mid // 2 :], upper)
+                for m in range(mid):
+                    put(out, base + mid * left + m, tiles[m])
+                    put(out, base + mid * (1 - left) + m, far[m])
+                row = iota(more[0].shape, 0)
+                nearer = (row >= HALF_ROWS) == upper
+                for m in range(NEAR_CORNER):
+                    put(out, base + (cx - NEAR_CORNER) * left + m, jnp.where(nearer, more[m], 0.0), add=True)
 
     got_sensors.wait()
     strips = [(j, None)]
@@ -255,34 +377,6 @@
                 for h in halves:
                     inject[t, xs, h, at] = value[:, :, half * h : half * (h + 1)]
 
-    for copy in got_fields + got_halos:
-        copy.wait()
-    for ref, left in ((odd_ref, 1 - parity), (even_ref, parity)):
-        base = 2 * cx * (1 - left)
-        at = 0
-        for out, count in zip(ext, plane_counts(cx)):
-            first = base + left if count < cx else base
-            for h in halves:
-                lanes = slice(half * h, half * (h + 1))
-                out[pl.ds(first, count), h, own_rows] = ref[at : at + count, :, lanes].astype(F32)
-            at += count
-        near = base + (cx - NEAR) * left
-        for out in ext:
-            for h in halves:
-                lanes = slice(half * h, half * (h + 1))
-                out[pl.ds(near, NEAR), h, own_rows] += ref[at : at + NEAR, :, lanes].astype(F32)
-            at += NEAR
-    for n in range(len(sides)):
-        for f, out in enumerate(ext):
-            for ref, left in ((corner_refs[2 * n], 1 - parity), (corner_refs[2 * n + 1], parity)):
-                corner = ref[f].astype(F32).reshape(cx + NEAR_CORNER, reach, nz)
-                base = 2 * cx * (1 - left)
-                near = base + (cx - NEAR_CORNER) * left
-                for h in halves:
-                    lanes, at = slice(half * h, half * (h + 1)), pl.ds(halo[n], reach)
-                    out[pl.ds(base, cx), h, at] = corner[:cx, :, lanes]
-                    out[pl.ds(near, NEAR_CORNER), h, at] += corner[cx:, :, lanes]
-
     lane = iota((rows, half), 1)
     last, first = lane == half - 1, lane == 0
     mid, above, below = slice(pad, pad + rows), slice(pad + 1, pad + rows + 1), slice(pad - 1, pad + rows - 1)
@@ -401,24 +495,38 @@
     fields = (adjoint_now, density, adjoint_last, velocity)
 
     planes = sum(plane_counts(cx)) + 4 * NEAR
-    prep_out = [shape((planes, cy, nz), BF16)] * 2
+    halo_block = shape((planes, cy, nz), BF16)
+    prep_out = [halo_block]
     for _ in sides:
-        prep_out += [shape((4, cx, reach, nz), F32)] + [shape((4, (cx + NEAR_CORNER) * reach, nz), BF16)] * 2
-    prep = call(functools.partial(prep_kernel, n_gy, reach), prep_out, fields)
+        prep_out += [shape((4, cx, reach, nz), F32)] + [shape((4 * reach * corner_tiles(cx), nz), BF16)] * 2
+    sensor_args = (
+        residual_panels,
+        owner_slab.reshape(1, sensors),
+        receiver_cell.reshape(1, sensors),
+        trace_offset.reshape(1, sensors),
+    )
+    stage_args = sensor_args + fields
+    stage_out = [shape((n_gx, n_gy, 8, 128), F32)] + prep_out
+    odd_send = call(
+        odd_kernel,
+        halo_block,
+        fields,
+        [pltpu.VMEM(x.shape, x.dtype) for x in (*fields, halo_block)] + [pltpu.SemaphoreType.DMA((8,))],
+        in_specs=[HBM] * 4,
+        out_specs=ANY,
+    )
+    packed, *prep = call(
+        functools.partial(stage_kernel, n_gx, n_gy, steps, slots, reach),
+        stage_out,
+        stage_args,
+        [pltpu.VMEM(x.shape, x.dtype) for x in (*stage_args, *stage_out)] + [pltpu.SemaphoreType.DMA((32,))],
+        in_specs=[HBM] * len(stage_args),
+        out_specs=[ANY] * len(stage_out),
+    )
     odd = [(a, a + 1) for a in range(1, n_gx - 1, 2)]
     odd = odd + [(b, a) for a, b in odd]
     even = [(a, a ^ 1) for a in range(n_gx)]
-    packed = call(
-        functools.partial(pack_kernel, n_gx, n_gy, steps, slots),
-        shape((n_gx, n_gy, 8, 128), F32),
-        (
-            residual_panels,
-            owner_slab.reshape(1, sensors),
-            receiver_cell.reshape(1, sensors),
-            trace_offset.reshape(1, sensors),
-        ),
-    )
-    odd_got = lax.ppermute(prep[0], "gx", odd)
+    odd_got = lax.ppermute(odd_send, "gx", odd)
     side_got = []
     for n, side in enumerate(sides):
         if side == "swap":
@@ -428,12 +536,12 @@
         else:
             over_y = [(b, b + 1) for b in range(n_gy - 1)]
         corner = [(a * n_gy + c, b * n_gy + d) for a, b in odd for c, d in over_y]
-        own_side = lax.ppermute(prep[2 + 3 * n], "gy", over_y)
-        odd_side = lax.ppermute(prep[3 + 3 * n], ("gx", "gy"), corner)
+        own_side = lax.ppermute(prep[1 + 3 * n], "gy", over_y)
+        odd_side = lax.ppermute(prep[2 + 3 * n], ("gx", "gy"), corner)
         corner = [(a * n_gy + c, b * n_gy + d) for a, b in even for c, d in over_y]
-        even_side = lax.ppermute(prep[4 + 3 * n], ("gx", "gy"), corner)
+        even_side = lax.ppermute(prep[3 + 3 * n], ("gx", "gy"), corner)
         side_got.append((own_side, even_side, odd_side))
-    even_got = lax.ppermute(prep[1], "gx", even)
+    even_got = lax.ppermute(prep[0], "gx", even)
 
     arrived = lax.all_to_all(
         packed.reshape(n_gx * n_gy, 8, 128), ("gx", "gy"), split_axis=0, concat_axis=0, tiled=True
@@ -459,7 +567,7 @@
         + [pltpu.SemaphoreType.DMA((64,))],
         in_specs=[HBM] * 5 + [ANY] * (3 + len(side_args)),
         out_specs=[HBM] + [VMEM] * len(outs),
-        limit=36 << 20,
+        limit=50 << 20,
     )
     if n_gy == 2:
         final, mine, send = got

time: 47.1 us -> 42.9 us (0.911)
  waiting for transfers between devices: 13 us -> 10.5 us
  local copies, waits for them, and re-layouts: 1.24 us -> 0.03 us
    all_to_all x1, waiting for transfers between devices: 4.2 us -> 2.51 us  [shards(): lax.all_to_all(packed.reshape(n_gx * n_gy, 8, 128), ('gx', 'gy'), split_a...]
    unnamed x10 -> x8, local copies, waits for them, and re-layouts: 1.24 us -> 0.03 us
    ppermute x5, waiting for transfers between devices: 4.94 us -> 4.11 us  [the longest x1 2.67 us: shards(): odd_side = lax.ppermute(prep[2 + 3 * n], ('gx', 'gy'), corner)]
  transfers between devices with their start and end apart: 7 -> 7, of which waited for: 4 -> 4; matrix products, arithmetic and copies ran while one was open for 0% -> 0% of each run, Pallas kernels for 6% -> 8%
where the time goes in v3:
time: 42.9 us; the launch traced here: 42.7 us
  Pallas kernels  16.7 us (39%)
  starting transfers between devices  14.1 us (33%)
  waiting for transfers between devices  10.5 us (24%)
  between operations  0.75 us (2%)
  other arithmetic  0.64 us (1%)
    pallas_call x3, Pallas kernels, call(): pl.pallas_call(kernel, out_shape=out_shape, in_specs=in_specs or [VMEM] *...  16.7 us
    all_to_all x1, starting transfers between devices, shards(): lax.all_to_all(packed.reshape(n_gx * n_gy, 8, 128), ('gx', 'gy'), split_a...  4.93 us
    ppermute x1, starting transfers between devices, shards(): odd_side = lax.ppermute(prep[2 + 3 * n], ('gx', 'gy'), corner)  4.21 us
    ppermute x1, waiting for transfers between devices, shards(): whole = mine + lax.ppermute(send, 'gy', [(0, 1), (1, 0)])  3.84 us
    ppermute x1, starting transfers between devices, shards(): odd_got = lax.ppermute(odd_send, 'gx', odd)  2.75 us
    ppermute x1, waiting for transfers between devices, shards(): odd_side = lax.ppermute(prep[2 + 3 * n], ('gx', 'gy'), corner)  2.67 us
    all_to_all x1, waiting for transfers between devices, shards(): lax.all_to_all(packed.reshape(n_gx * n_gy, 8, 128), ('gx', 'gy'), split_a...  2.51 us
    ppermute x1, waiting for transfers between devices, shards(): even_side = lax.ppermute(prep[3 + 3 * n], ('gx', 'gy'), corner)  1.43 us
  transfers between devices with their start and end apart: 7, of which 4 were waited for; matrix products, arithmetic and copies ran while one was open for 0% of the time, Pallas kernels for 8%

profile of v3, /device:TPU:26, one launch (start us, length us, event | category | flops | bytes accessed | tf_op | source)
XLA Modules:
  0.0 42.7 jit_solution(6621275463809228212)
XLA Ops:
  0.6 1.9 %shard_map.105 = bf16[42,32,256]{2,1,0:T(8,128)(2,1)} custom-call(f32[8,32,256]{2,1,0:T(8,128)} %refs_0_.5, f32[8,32,256]{2,1,0:T(8,128)} %refs_1_.3, f32[8,32,256]{2,1,0:T(8,128)} %refs_2_.3, f32[8,32,256]{2,1,0:T(8,128)} %refs_3_.3), custom_call_target="tpu_custom_call" | custom-call | tf_op jit(solution)/shard_map/pallas_call | solution.py:465
  2.6 2.8 %collective-permute-start = (bf16[42,32,256]{2,1,0:T(8,128)(2,1)}, bf16[42,32,256]{2,1,0:T(8,128)(2,1)S(1)}, u32[]{:S(2)}, u32[]{:S(2)}) collective-permute-start(bf16[42,32,256]{2,1,0:T(8,128)(2,1)} %shard_map.105), channel_id=1, source_target_pairs={{2,4},{6,8},{10,12},{14,16},{18,20},{22,24},{26,28},{4,2},{8,6},{1... | collective-permute-start | bytes 2064392 | tf_op jit(solution)/shard_map/ppermute | solution.py:529
  5.3 0.0 copy-start.1
  5.4 0.0 copy-start.2
  5.4 0.0 copy-start.3
  5.4 3.4 %shard_map.104 = (f32[16,2,8,128]{3,2,1,0:T(8,128)}, bf16[42,32,256]{2,1,0:T(8,128)(2,1)}, f32[4,8,8,256]{3,2,1,0:T(8,128)}, bf16[224,256]{1,0:T(8,128)(2,1)}, bf16[224,256]{1,0:T(8,128)(2,1)}) custom-call(bf16[512,128]{1,0:T(8,128)(2,1)} %refs_0_.3, s32[1,512]{1,0:T(1,128)} %bitcast.9, s32[1,512]{1,0:T(1,128)} %bitcast.10, s32[1,512]{1,0:T(1,128)} %bitcast.11, ...), custom_call_target="tpu_custom_call" | custom-call | tf_op jit(solution)/shard_map/pallas_call | solution.py:465
  8.8 0.0 copy-start
  8.8 0.9 %collective-permute-start.1 = (bf16[42,32,256]{2,1,0:T(8,128)(2,1)}, bf16[42,32,256]{2,1,0:T(8,128)(2,1)S(1)}, u32[]{:S(2)}, u32[]{:S(2)}) collective-permute-start(bf16[42,32,256]{2,1,0:T(8,128)(2,1)} %get-tuple-element.11), channel_id=1, source_target_pairs={{0,2},{2,0},{4,6},{6,4},{8,10},{10,8},{12,14},{14,12},{16,18},{18,... | collective-permute-start | bytes 2064392 | tf_op jit(solution)/shard_map/ppermute | solution.py:544
  9.7 0.5 %collective-permute-start.2 = (f32[4,8,8,256]{3,2,1,0:T(8,128)}, f32[4,8,8,256]{3,2,1,0:T(8,128)S(1)}, u32[]{:S(2)}, u32[]{:S(2)}) collective-permute-start(f32[4,8,8,256]{3,2,1,0:T(8,128)} %get-tuple-element.12), channel_id=1, source_target_pairs={{0,1},{1,0},{2,3},{3,2},{4,5},{5,4},{6,7},{7,6},{8,9},{9,8},{10,11... | collective-permute-start | bytes 786440 | tf_op jit(solution)/shard_map/ppermute | solution.py:539
  10.2 4.9 %all-to-all-start = ((f32[32,8,128]{2,1,0:T(8,128)}), f32[32,8,128]{2,1,0:T(8,128)S(1)}, u32[]{:S(2)}, u32[]{:S(2)}) async-start(f32[32,8,128]{2,1,0:T(8,128)} %bitcast.8), calls=%async_computation | async-start | bytes 262144 | tf_op jit(solution)/shard_map/all_to_all | solution.py:546
  15.2 0.4 collective-permute-start.3
  15.5 4.2 %collective-permute-start.4 = (bf16[224,256]{1,0:T(8,128)(2,1)}, bf16[224,256]{1,0:T(8,128)(2,1)S(1)}, u32[]{:S(2)}, u32[]{:S(2)}) collective-permute-start(bf16[224,256]{1,0:T(8,128)(2,1)} %get-tuple-element.14), channel_id=1, source_target_pairs={{2,5},{3,4},{6,9},{7,8},{10,13},{11,12},{14,17},{15,16},{18,21},{1... | collective-permute-start | bytes 344072 | tf_op jit(solution)/shard_map/ppermute | solution.py:540
  19.8 1.4 %collective-permute-done.3.refs_9_ = bf16[224,256]{1,0:T(8,128)(2,1)S(1)} collective-permute-done((bf16[224,256]{1,0:T(8,128)(2,1)}, bf16[224,256]{1,0:T(8,128)(2,1)S(1)}, u32[]{:S(2)}, u32[]{:S(2)}) %collective-permute-start.3) | collective-permute-done | bytes 114720 | tf_op jit(solution)/shard_map/ppermute | solution.py:542
  21.2 2.7 %collective-permute-done.4.refs_10_ = bf16[224,256]{1,0:T(8,128)(2,1)S(1)} collective-permute-done((bf16[224,256]{1,0:T(8,128)(2,1)}, bf16[224,256]{1,0:T(8,128)(2,1)S(1)}, u32[]{:S(2)}, u32[]{:S(2)}) %collective-permute-start.4) | collective-permute-done | bytes 114720 | tf_op jit(solution)/shard_map/ppermute | solution.py:540
  23.9 2.5 %all-to-all-done = f32[32,8,128]{2,1,0:T(8,128)S(1)} async-done(((f32[32,8,128]{2,1,0:T(8,128)}), f32[32,8,128]{2,1,0:T(8,128)S(1)}, u32[]{:S(2)}, u32[]{:S(2)}) %all-to-all-start) | async-done | bytes 131104 | tf_op jit(solution)/shard_map/all_to_all | solution.py:546
  26.4 0.0 collective-permute-done.2.refs_8_
  26.4 0.0 collective-permute-done.refs_6_
  26.4 0.0 collective-permute-done.1.refs_7_
  26.4 0.0 copy-done.1
  26.4 0.0 copy-done.2
  26.4 0.0 copy-done.3
  26.4 0.0 copy-done
  26.4 11.3 %shard_map.106 = (f32[8,32,256]{2,1,0:T(8,128)}, f32[4,32,64]{2,1,0:T(8,128)S(1)}, f32[4,32,64]{2,1,0:T(8,128)S(1)}) custom-call(f32[8,32,256]{2,1,0:T(8,128)S(1)} %copy-done, f32[8,32,256]{2,1,0:T(8,128)S(1)} %copy-done.1, f32[8,32,256]{2,1,0:T(8,128)S(1)} %copy-done.2, f32[8,32,256]{2,1,0:T(8,128)S(1)} %copy-done.3, bf16[8,8,32,256]{3,2,1,0:T(8,128)(2,1)} %refs_4_.3, ...), custom_call_target="tpu_custom_call" | custom-call | tf_op jit(solution)/shard_map/pallas_call | solution.py:465
  37.7 0.5 %collective-permute-start.5 = (f32[4,32,64]{2,1,0:T(8,128)S(1)}, f32[4,32,64]{2,1,0:T(8,128)S(1)}, u32[]{:S(2)}, u32[]{:S(2)}) collective-permute-start(f32[4,32,64]{2,1,0:T(8,128)S(1)} %get-tuple-element.16), channel_id=1, source_target_pairs={{0,1},{1,0},{2,3},{3,2},{4,5},{5,4},{6,7},{7,6},{8,9},{9,8},{10,11... | collective-permute-start | bytes 98312 | tf_op jit(solution)/shard_map/ppermute | solution.py:574
  38.2 3.8 %collective-permute-done.5 = f32[4,32,64]{2,1,0:T(8,128)S(1)} collective-permute-done((f32[4,32,64]{2,1,0:T(8,128)S(1)}, f32[4,32,64]{2,1,0:T(8,128)S(1)}, u32[]{:S(2)}, u32[]{:S(2)}) %collective-permute-start.5) | collective-permute-done | bytes 32800 | tf_op jit(solution)/shard_map/ppermute | solution.py:574
  42.1 0.6 %add_bitcast_fusion = f32[4,64,32]{1,2,0:T(8,128)} fusion(f32[4,32,64]{2,1,0:T(8,128)S(1)} %get-tuple-element.15, f32[4,32,64]{2,1,0:T(8,128)S(1)} %collective-permute-done.5), kind=kLoop, calls=%fused_computation | loop fusion | flops 8192 | bytes 98304 | tf_op jit(solution)/shard_map/transpose | solution.py:575
Async XLA Ops:
  2.6 23.8 %collective-permute-start = (bf16[42,32,256]{2,1,0:T(8,128)(2,1)}, bf16[42,32,256]{2,1,0:T(8,128)(2,1)S(1)}, u32[]{:S(2)}, u32[]{:S(2)}) collective-permute-start(bf16[42,32,256]{2,1,0:T(8,128)(2,1)} %shard_map.105), channel_id=1, source_target_pairs={{2,4},{6,8},{10,12},{14,16},{18,20},{22,24},{26,28},{4,2},{8,6},{1... | collective-permute-start | bytes 2064392 | tf_op jit(solution)/shard_map/ppermute | solution.py:529
  5.3 21.0 %copy-start.1 = (f32[8,32,256]{2,1,0:T(8,128)S(1)}, f32[8,32,256]{2,1,0:T(8,128)}, u32[]{:S(2)}) copy-start(f32[8,32,256]{2,1,0:T(8,128)} %refs_1_.3) | copy-start | bytes 786436
  5.4 21.0 %copy-start.2 = (f32[8,32,256]{2,1,0:T(8,128)S(1)}, f32[8,32,256]{2,1,0:T(8,128)}, u32[]{:S(2)}) copy-start(f32[8,32,256]{2,1,0:T(8,128)} %refs_2_.3) | copy-start | bytes 786436
  5.4 21.0 %copy-start.3 = (f32[8,32,256]{2,1,0:T(8,128)S(1)}, f32[8,32,256]{2,1,0:T(8,128)}, u32[]{:S(2)}) copy-start(f32[8,32,256]{2,1,0:T(8,128)} %refs_3_.3) | copy-start | bytes 786436
  8.8 17.6 %copy-start = (f32[8,32,256]{2,1,0:T(8,128)S(1)}, f32[8,32,256]{2,1,0:T(8,128)}, u32[]{:S(2)}) copy-start(f32[8,32,256]{2,1,0:T(8,128)} %refs_0_.5) | copy-start | bytes 786436
  8.8 17.5 %collective-permute-start.1 = (bf16[42,32,256]{2,1,0:T(8,128)(2,1)}, bf16[42,32,256]{2,1,0:T(8,128)(2,1)S(1)}, u32[]{:S(2)}, u32[]{:S(2)}) collective-permute-start(bf16[42,32,256]{2,1,0:T(8,128)(2,1)} %get-tuple-element.11), channel_id=1, source_target_pairs={{0,2},{2,0},{4,6},{6,4},{8,10},{10,8},{12,14},{14,12},{16,18},{18,... | collective-permute-start | bytes 2064392 | tf_op jit(solution)/shard_map/ppermute | solution.py:544
  9.7 16.7 %collective-permute-start.2 = (f32[4,8,8,256]{3,2,1,0:T(8,128)}, f32[4,8,8,256]{3,2,1,0:T(8,128)S(1)}, u32[]{:S(2)}, u32[]{:S(2)}) collective-permute-start(f32[4,8,8,256]{3,2,1,0:T(8,128)} %get-tuple-element.12), channel_id=1, source_target_pairs={{0,1},{1,0},{2,3},{3,2},{4,5},{5,4},{6,7},{7,6},{8,9},{9,8},{10,11... | collective-permute-start | bytes 786440 | tf_op jit(solution)/shard_map/ppermute | solution.py:539
  10.2 16.1 %all-to-all-start = ((f32[32,8,128]{2,1,0:T(8,128)}), f32[32,8,128]{2,1,0:T(8,128)S(1)}, u32[]{:S(2)}, u32[]{:S(2)}) async-start(f32[32,8,128]{2,1,0:T(8,128)} %bitcast.8), calls=%async_computation | async-start | bytes 262144 | tf_op jit(solution)/shard_map/all_to_all | solution.py:546
  15.2 6.0 %collective-permute-start.3 = (bf16[224,256]{1,0:T(8,128)(2,1)}, bf16[224,256]{1,0:T(8,128)(2,1)S(1)}, u32[]{:S(2)}, u32[]{:S(2)}) collective-permute-start(bf16[224,256]{1,0:T(8,128)(2,1)} %get-tuple-element.13), channel_id=1, source_target_pairs={{0,3},{1,2},{2,1},{3,0},{4,7},{5,6},{6,5},{7,4},{8,11},{9,10},{10,... | collective-permute-start | bytes 344072 | tf_op jit(solution)/shard_map/ppermute | solution.py:542
  15.5 8.3 %collective-permute-start.4 = (bf16[224,256]{1,0:T(8,128)(2,1)}, bf16[224,256]{1,0:T(8,128)(2,1)S(1)}, u32[]{:S(2)}, u32[]{:S(2)}) collective-permute-start(bf16[224,256]{1,0:T(8,128)(2,1)} %get-tuple-element.14), channel_id=1, source_target_pairs={{2,5},{3,4},{6,9},{7,8},{10,13},{11,12},{14,17},{15,16},{18,21},{1... | collective-permute-start | bytes 344072 | tf_op jit(solution)/shard_map/ppermute | solution.py:540
  37.7 4.3 %collective-permute-start.5 = (f32[4,32,64]{2,1,0:T(8,128)S(1)}, f32[4,32,64]{2,1,0:T(8,128)S(1)}, u32[]{:S(2)}, u32[]{:S(2)}) collective-permute-start(f32[4,32,64]{2,1,0:T(8,128)S(1)} %get-tuple-element.16), channel_id=1, source_target_pairs={{0,1},{1,0},{2,3},{3,2},{4,5},{5,4},{6,7},{7,6},{8,9},{9,8},{10,11... | collective-permute-start | bytes 98312 | tf_op jit(solution)/shard_map/ppermute | solution.py:574

commit v4 on v3

--- a/solution.py
+++ b/solution.py
@@ -299,14 +299,21 @@
         codes = jnp.concatenate(codes, axis=1)
         return [jnp.concatenate(t, axis=1) for t in tiles], codes.astype(I32) - 1, jnp.transpose(codes).astype(I32) - 1
 
-    def spread(cells_at, amps, column, spans):
+    def spread(cells_at, amps, column, spans, near_spans):
         depth = one_hot(iota((width, nz), 1) == (column & (nz - 1)))
-        hi, lo = parts_of(amps, 2)
-        out = 0.0
-        for part in (lo, hi):
-            block = jnp.concatenate([cells_at[a:b] * part[t : t + 1] for t, a, b in spans], axis=0)
-            out = out + jnp.dot(block, depth, preferred_element_type=F32)
-        return out
+        outs = []
+        for part, chosen in zip(parts_of(amps, 2), (spans, near_spans)):
+            block = jnp.concatenate([cells_at[a:b] * part[t : t + 1] for t, a, b in chosen], axis=0)
+            outs.append(jnp.dot(block, depth, preferred_element_type=F32))
+        values, first, first_near = [], 0, 0
+        nearer = {t: (a, b) for t, a, b in near_spans}
+        for t, a, b in spans:
+            c, d = nearer[t]
+            x = outs[0][first : first + b - a]
+            y = x[c - a : d - a] + outs[1][first_near : first_near + d - c]
+            values.append(jnp.concatenate([z for z in (x[: c - a], y, x[d - a :]) if z.shape[0]], axis=0))
+            first, first_near = first + b - a, first_near + d - c
+        return values
 
     for copy in got_fields + got_halos:
         copy.wait()
@@ -368,11 +375,11 @@
             cells = one_hot(iota((cx * tall, width), 0) == place)
             layers = [(max(t + 1 - cx * slab, 0), min(3 * cx - 1 - t - cx * slab, cx)) for t in range(steps)]
             spans = [(t, a * tall, b * tall) for t, (a, b) in enumerate(layers) if a < b]
-            out = spread(cells, amps[slab], columns[:, slab : slab + 1], spans)
-            first = 0
-            for t, a, b in spans:
-                value = out[first : first + b - a].reshape((b - a) // tall, tall, nz)
-                first += b - a
+            low, high = ((cx - NEAR) * tall, cx * tall) if slab == 0 else (0, (cx if slab == 1 else NEAR) * tall)
+            near_spans = [(t, min(max(a, low), b), max(min(b, high), a)) for t, a, b in spans]
+            values = spread(cells, amps[slab], columns[:, slab : slab + 1], spans, near_spans)
+            for (t, a, b), value in zip(spans, values):
+                value = value.reshape((b - a) // tall, tall, nz)
                 xs = slice(slab * cx + a // tall, slab * cx + b // tall)
                 for h in halves:
                     inject[t, xs, h, at] = value[:, :, half * h : half * (h + 1)]
@@ -412,22 +419,24 @@
     wave, prev = w_ref, prev_ref
     for t in range(steps):
 
-        def advance(x, wave=wave, prev=prev, t=t):
-            w = [wave[x, h, mid] for h in halves]
+        def advance(x, w, behind, wave=wave, prev=prev, t=t):
+            ahead = [wave[x + 1, h, mid] for h in halves]
             deep, shallow = shifted(*w)
             for h in halves:
                 u = c0[x, h] * w[h] - prev[x, h, mid] + inject[t, x, h]
-                u = u + (cxu[x, h] * wave[x + 1, h, mid] + cxd[x, h] * wave[x - 1, h, mid])
+                u = u + (cxu[x, h] * ahead[h] + cxd[x, h] * behind[h])
                 u = u + (cyu[x, h] * wave[x, h, above] + cyd[x, h] * wave[x, h, below])
                 prev[x, h, mid] = u + (czu[x, h] * deep[h] + czd[x, h] * shallow[h])
+            return ahead, w
 
         def gather(x, prev=prev, t=t):
             for h in halves:
                 term = prev[cx + x, h, own_rows] * forward_ref[t, x, :, half * h : half * (h + 1)].astype(F32)
                 acc_ref[x, h] = term if t == 0 else acc_ref[x, h] + term
 
+        at, behind = [wave[t + 1, h, mid] for h in halves], [wave[t, h, mid] for h in halves]
         for x in range(t + 1, 3 * cx - 1 - t):
-            advance(x)
+            at, behind = advance(x, at, behind)
             if cx <= x < 2 * cx:
                 gather(x - cx)
         wave, prev = prev, wave

time: 42.9 us -> 42.3 us (0.986)
  Pallas kernels: 16.7 us -> 16.1 us
    pallas_call x3, Pallas kernels: 16.7 us -> 16.1 us  [call(): pl.pallas_call(kernel, out_shape=out_shape, in_specs=in_specs or [VMEM] *...]
where the time goes in v4:
time: 42.3 us; the launch traced here: 42.1 us
  Pallas kernels  16.1 us (38%)
  starting transfers between devices  14.1 us (33%)
  waiting for transfers between devices  10.4 us (25%)
  between operations  0.75 us (2%)
  other arithmetic  0.64 us (2%)
    pallas_call x3, Pallas kernels, call(): pl.pallas_call(kernel, out_shape=out_shape, in_specs=in_specs or [VMEM] *...  16.1 us
    all_to_all x1, starting transfers between devices, shards(): lax.all_to_all(packed.reshape(n_gx * n_gy, 8, 128), ('gx', 'gy'), split_a...  4.93 us
    ppermute x1, starting transfers between devices, shards(): odd_side = lax.ppermute(prep[2 + 3 * n], ('gx', 'gy'), corner)  4.21 us
    ppermute x1, waiting for transfers between devices, shards(): whole = mine + lax.ppermute(send, 'gy', [(0, 1), (1, 0)])  3.83 us
    ppermute x1, starting transfers between devices, shards(): odd_got = lax.ppermute(odd_send, 'gx', odd)  2.75 us
    ppermute x1, waiting for transfers between devices, shards(): odd_side = lax.ppermute(prep[2 + 3 * n], ('gx', 'gy'), corner)  2.67 us
    all_to_all x1, waiting for transfers between devices, shards(): lax.all_to_all(packed.reshape(n_gx * n_gy, 8, 128), ('gx', 'gy'), split_a...  2.51 us
    ppermute x1, waiting for transfers between devices, shards(): even_side = lax.ppermute(prep[3 + 3 * n], ('gx', 'gy'), corner)  1.43 us
  transfers between devices with their start and end apart: 7, of which 4 were waited for; matrix products, arithmetic and copies ran while one was open for 0% of the time, Pallas kernels for 8%

profile of v4, /device:TPU:26, one launch (start us, length us, event | category | flops | bytes accessed | tf_op | source)
XLA Modules:
  0.0 42.1 jit_solution(14535968834495638018)
XLA Ops:
  0.6 1.9 %shard_map.105 = bf16[42,32,256]{2,1,0:T(8,128)(2,1)} custom-call(f32[8,32,256]{2,1,0:T(8,128)} %refs_0_.5, f32[8,32,256]{2,1,0:T(8,128)} %refs_1_.3, f32[8,32,256]{2,1,0:T(8,128)} %refs_2_.3, f32[8,32,256]{2,1,0:T(8,128)} %refs_3_.3), custom_call_target="tpu_custom_call" | custom-call | tf_op jit(solution)/shard_map/pallas_call | solution.py:474
  2.6 2.8 %collective-permute-start = (bf16[42,32,256]{2,1,0:T(8,128)(2,1)}, bf16[42,32,256]{2,1,0:T(8,128)(2,1)S(1)}, u32[]{:S(2)}, u32[]{:S(2)}) collective-permute-start(bf16[42,32,256]{2,1,0:T(8,128)(2,1)} %shard_map.105), channel_id=1, source_target_pairs={{2,4},{6,8},{10,12},{14,16},{18,20},{22,24},{26,28},{4,2},{8,6},{1... | collective-permute-start | bytes 2064392 | tf_op jit(solution)/shard_map/ppermute | solution.py:538
  5.3 0.0 copy-start.1
  5.4 0.0 copy-start.2
  5.4 0.0 copy-start.3
  5.4 3.4 %shard_map.104 = (f32[16,2,8,128]{3,2,1,0:T(8,128)}, bf16[42,32,256]{2,1,0:T(8,128)(2,1)}, f32[4,8,8,256]{3,2,1,0:T(8,128)}, bf16[224,256]{1,0:T(8,128)(2,1)}, bf16[224,256]{1,0:T(8,128)(2,1)}) custom-call(bf16[512,128]{1,0:T(8,128)(2,1)} %refs_0_.3, s32[1,512]{1,0:T(1,128)} %bitcast.9, s32[1,512]{1,0:T(1,128)} %bitcast.10, s32[1,512]{1,0:T(1,128)} %bitcast.11, ...), custom_call_target="tpu_custom_call" | custom-call | tf_op jit(solution)/shard_map/pallas_call | solution.py:474
  8.8 0.0 copy-start
  8.8 0.9 %collective-permute-start.1 = (bf16[42,32,256]{2,1,0:T(8,128)(2,1)}, bf16[42,32,256]{2,1,0:T(8,128)(2,1)S(1)}, u32[]{:S(2)}, u32[]{:S(2)}) collective-permute-start(bf16[42,32,256]{2,1,0:T(8,128)(2,1)} %get-tuple-element.11), channel_id=1, source_target_pairs={{0,2},{2,0},{4,6},{6,4},{8,10},{10,8},{12,14},{14,12},{16,18},{18,... | collective-permute-start | bytes 2064392 | tf_op jit(solution)/shard_map/ppermute | solution.py:553
  9.7 0.5 %collective-permute-start.2 = (f32[4,8,8,256]{3,2,1,0:T(8,128)}, f32[4,8,8,256]{3,2,1,0:T(8,128)S(1)}, u32[]{:S(2)}, u32[]{:S(2)}) collective-permute-start(f32[4,8,8,256]{3,2,1,0:T(8,128)} %get-tuple-element.12), channel_id=1, source_target_pairs={{0,1},{1,0},{2,3},{3,2},{4,5},{5,4},{6,7},{7,6},{8,9},{9,8},{10,11... | collective-permute-start | bytes 786440 | tf_op jit(solution)/shard_map/ppermute | solution.py:548
  10.2 4.9 %all-to-all-start = ((f32[32,8,128]{2,1,0:T(8,128)}), f32[32,8,128]{2,1,0:T(8,128)S(1)}, u32[]{:S(2)}, u32[]{:S(2)}) async-start(f32[32,8,128]{2,1,0:T(8,128)} %bitcast.8), calls=%async_computation | async-start | bytes 262144 | tf_op jit(solution)/shard_map/all_to_all | solution.py:555
  15.2 0.4 collective-permute-start.3
  15.5 4.2 %collective-permute-start.4 = (bf16[224,256]{1,0:T(8,128)(2,1)}, bf16[224,256]{1,0:T(8,128)(2,1)S(1)}, u32[]{:S(2)}, u32[]{:S(2)}) collective-permute-start(bf16[224,256]{1,0:T(8,128)(2,1)} %get-tuple-element.14), channel_id=1, source_target_pairs={{2,5},{3,4},{6,9},{7,8},{10,13},{11,12},{14,17},{15,16},{18,21},{1... | collective-permute-start | bytes 344072 | tf_op jit(solution)/shard_map/ppermute | solution.py:549
  19.8 1.4 %collective-permute-done.3.refs_9_ = bf16[224,256]{1,0:T(8,128)(2,1)S(1)} collective-permute-done((bf16[224,256]{1,0:T(8,128)(2,1)}, bf16[224,256]{1,0:T(8,128)(2,1)S(1)}, u32[]{:S(2)}, u32[]{:S(2)}) %collective-permute-start.3) | collective-permute-done | bytes 114720 | tf_op jit(solution)/shard_map/ppermute | solution.py:551
  21.2 2.7 %collective-permute-done.4.refs_10_ = bf16[224,256]{1,0:T(8,128)(2,1)S(1)} collective-permute-done((bf16[224,256]{1,0:T(8,128)(2,1)}, bf16[224,256]{1,0:T(8,128)(2,1)S(1)}, u32[]{:S(2)}, u32[]{:S(2)}) %collective-permute-start.4) | collective-permute-done | bytes 114720 | tf_op jit(solution)/shard_map/ppermute | solution.py:549
  23.9 2.5 %all-to-all-done = f32[32,8,128]{2,1,0:T(8,128)S(1)} async-done(((f32[32,8,128]{2,1,0:T(8,128)}), f32[32,8,128]{2,1,0:T(8,128)S(1)}, u32[]{:S(2)}, u32[]{:S(2)}) %all-to-all-start) | async-done | bytes 131104 | tf_op jit(solution)/shard_map/all_to_all | solution.py:555
  26.4 0.0 collective-permute-done.2.refs_8_
  26.4 0.0 collective-permute-done.refs_6_
  26.4 0.0 collective-permute-done.1.refs_7_
  26.4 0.0 copy-done.1
  26.4 0.0 copy-done.2
  26.4 0.0 copy-done.3
  26.4 0.0 copy-done
  26.4 10.7 %shard_map.106 = (f32[8,32,256]{2,1,0:T(8,128)}, f32[4,32,64]{2,1,0:T(8,128)S(1)}, f32[4,32,64]{2,1,0:T(8,128)S(1)}) custom-call(f32[8,32,256]{2,1,0:T(8,128)S(1)} %copy-done, f32[8,32,256]{2,1,0:T(8,128)S(1)} %copy-done.1, f32[8,32,256]{2,1,0:T(8,128)S(1)} %copy-done.2, f32[8,32,256]{2,1,0:T(8,128)S(1)} %copy-done.3, bf16[8,8,32,256]{3,2,1,0:T(8,128)(2,1)} %refs_4_.3, ...), custom_call_target="tpu_custom_call" | custom-call | tf_op jit(solution)/shard_map/pallas_call | solution.py:474
  37.1 0.5 %collective-permute-start.5 = (f32[4,32,64]{2,1,0:T(8,128)S(1)}, f32[4,32,64]{2,1,0:T(8,128)S(1)}, u32[]{:S(2)}, u32[]{:S(2)}) collective-permute-start(f32[4,32,64]{2,1,0:T(8,128)S(1)} %get-tuple-element.16), channel_id=1, source_target_pairs={{0,1},{1,0},{2,3},{3,2},{4,5},{5,4},{6,7},{7,6},{8,9},{9,8},{10,11... | collective-permute-start | bytes 98312 | tf_op jit(solution)/shard_map/ppermute | solution.py:583
  37.6 3.8 %collective-permute-done.5 = f32[4,32,64]{2,1,0:T(8,128)S(1)} collective-permute-done((f32[4,32,64]{2,1,0:T(8,128)S(1)}, f32[4,32,64]{2,1,0:T(8,128)S(1)}, u32[]{:S(2)}, u32[]{:S(2)}) %collective-permute-start.5) | collective-permute-done | bytes 32800 | tf_op jit(solution)/shard_map/ppermute | solution.py:583
  41.5 0.6 %add_bitcast_fusion = f32[4,64,32]{1,2,0:T(8,128)} fusion(f32[4,32,64]{2,1,0:T(8,128)S(1)} %get-tuple-element.15, f32[4,32,64]{2,1,0:T(8,128)S(1)} %collective-permute-done.5), kind=kLoop, calls=%fused_computation | loop fusion | flops 8192 | bytes 98304 | tf_op jit(solution)/shard_map/transpose | solution.py:584
Async XLA Ops:
  2.6 23.8 %collective-permute-start = (bf16[42,32,256]{2,1,0:T(8,128)(2,1)}, bf16[42,32,256]{2,1,0:T(8,128)(2,1)S(1)}, u32[]{:S(2)}, u32[]{:S(2)}) collective-permute-start(bf16[42,32,256]{2,1,0:T(8,128)(2,1)} %shard_map.105), channel_id=1, source_target_pairs={{2,4},{6,8},{10,12},{14,16},{18,20},{22,24},{26,28},{4,2},{8,6},{1... | collective-permute-start | bytes 2064392 | tf_op jit(solution)/shard_map/ppermute | solution.py:538
  5.3 21.0 %copy-start.1 = (f32[8,32,256]{2,1,0:T(8,128)S(1)}, f32[8,32,256]{2,1,0:T(8,128)}, u32[]{:S(2)}) copy-start(f32[8,32,256]{2,1,0:T(8,128)} %refs_1_.3) | copy-start | bytes 786436
  5.4 21.0 %copy-start.2 = (f32[8,32,256]{2,1,0:T(8,128)S(1)}, f32[8,32,256]{2,1,0:T(8,128)}, u32[]{:S(2)}) copy-start(f32[8,32,256]{2,1,0:T(8,128)} %refs_2_.3) | copy-start | bytes 786436
  5.4 21.0 %copy-start.3 = (f32[8,32,256]{2,1,0:T(8,128)S(1)}, f32[8,32,256]{2,1,0:T(8,128)}, u32[]{:S(2)}) copy-start(f32[8,32,256]{2,1,0:T(8,128)} %refs_3_.3) | copy-start | bytes 786436
  8.8 17.6 %copy-start = (f32[8,32,256]{2,1,0:T(8,128)S(1)}, f32[8,32,256]{2,1,0:T(8,128)}, u32[]{:S(2)}) copy-start(f32[8,32,256]{2,1,0:T(8,128)} %refs_0_.5) | copy-start | bytes 786436
  8.8 17.5 %collective-permute-start.1 = (bf16[42,32,256]{2,1,0:T(8,128)(2,1)}, bf16[42,32,256]{2,1,0:T(8,128)(2,1)S(1)}, u32[]{:S(2)}, u32[]{:S(2)}) collective-permute-start(bf16[42,32,256]{2,1,0:T(8,128)(2,1)} %get-tuple-element.11), channel_id=1, source_target_pairs={{0,2},{2,0},{4,6},{6,4},{8,10},{10,8},{12,14},{14,12},{16,18},{18,... | collective-permute-start | bytes 2064392 | tf_op jit(solution)/shard_map/ppermute | solution.py:553
  9.7 16.7 %collective-permute-start.2 = (f32[4,8,8,256]{3,2,1,0:T(8,128)}, f32[4,8,8,256]{3,2,1,0:T(8,128)S(1)}, u32[]{:S(2)}, u32[]{:S(2)}) collective-permute-start(f32[4,8,8,256]{3,2,1,0:T(8,128)} %get-tuple-element.12), channel_id=1, source_target_pairs={{0,1},{1,0},{2,3},{3,2},{4,5},{5,4},{6,7},{7,6},{8,9},{9,8},{10,11... | collective-permute-start | bytes 786440 | tf_op jit(solution)/shard_map/ppermute | solution.py:548
  10.2 16.1 %all-to-all-start = ((f32[32,8,128]{2,1,0:T(8,128)}), f32[32,8,128]{2,1,0:T(8,128)S(1)}, u32[]{:S(2)}, u32[]{:S(2)}) async-start(f32[32,8,128]{2,1,0:T(8,128)} %bitcast.8), calls=%async_computation | async-start | bytes 262144 | tf_op jit(solution)/shard_map/all_to_all | solution.py:555
  15.2 6.0 %collective-permute-start.3 = (bf16[224,256]{1,0:T(8,128)(2,1)}, bf16[224,256]{1,0:T(8,128)(2,1)S(1)}, u32[]{:S(2)}, u32[]{:S(2)}) collective-permute-start(bf16[224,256]{1,0:T(8,128)(2,1)} %get-tuple-element.13), channel_id=1, source_target_pairs={{0,3},{1,2},{2,1},{3,0},{4,7},{5,6},{6,5},{7,4},{8,11},{9,10},{10,... | collective-permute-start | bytes 344072 | tf_op jit(solution)/shard_map/ppermute | solution.py:551
  15.5 8.3 %collective-permute-start.4 = (bf16[224,256]{1,0:T(8,128)(2,1)}, bf16[224,256]{1,0:T(8,128)(2,1)S(1)}, u32[]{:S(2)}, u32[]{:S(2)}) collective-permute-start(bf16[224,256]{1,0:T(8,128)(2,1)} %get-tuple-element.14), channel_id=1, source_target_pairs={{2,5},{3,4},{6,9},{7,8},{10,13},{11,12},{14,17},{15,16},{18,21},{1... | collective-permute-start | bytes 344072 | tf_op jit(solution)/shard_map/ppermute | solution.py:549
  37.1 4.3 %collective-permute-start.5 = (f32[4,32,64]{2,1,0:T(8,128)S(1)}, f32[4,32,64]{2,1,0:T(8,128)S(1)}, u32[]{:S(2)}, u32[]{:S(2)}) collective-permute-start(f32[4,32,64]{2,1,0:T(8,128)S(1)} %get-tuple-element.16), channel_id=1, source_target_pairs={{0,1},{1,0},{2,3},{3,2},{4,5},{5,4},{6,7},{7,6},{8,9},{9,8},{10,11... | collective-permute-start | bytes 98312 | tf_op jit(solution)/shard_map/ppermute | solution.py:583

commit v5 on v4

--- a/solution.py
+++ b/solution.py
@@ -79,10 +79,10 @@
     code = cell_ref[...] + 1
     line = iota((8, sensors), 0)
     code_rows = jnp.where(line == 0, code >> 8, jnp.where(line == 1, code & 255, 0))
-    rows = parts_of(amplitudes, 3) + [code_rows.astype(F32).astype(BF16)]
-    packed = [dot_t(part, moved) for part in rows]
-    packed_amp = packed[0] + packed[1] + packed[2]
-    packed_code = packed[3][0:1] * 256.0 + packed[3][1:2]
+    rows = [part.astype(F32) for part in parts_of(amplitudes, 3)] + [code_rows.astype(F32)]
+    packed = dot_t(jnp.concatenate(rows, axis=0).astype(BF16), moved)
+    packed_amp = packed[0:8] + packed[8:16] + packed[16:24]
+    packed_code = packed[24:25] * 256.0 + packed[25:26]
     blank = jnp.zeros((8, 128), F32)
     width = places + 128
     amp_pad = pltpu.roll(jnp.concatenate([packed_amp, blank], axis=1), slots, 1)
@@ -455,15 +455,20 @@
         flat = [jnp.where(j == h, flat[0], flat[1]) for h in halves]
     half_z = one_hot(iota((half, half // 2), 0) // 2 == iota((half, half // 2), 1))
     count = cx // 2 * cy
-    tall = count if n_gy == 2 else count // 2
-    to, at = iota((tall, count), 0), iota((tall, count), 1)
-    goal = at // cy * cy + j * (cy // 2) + at % cy // 2 if n_gy == 2 else at // 2
-    half_y = one_hot(to == goal)
+
+    def half_y(tall, goal):
+        return one_hot(iota((tall, count), 0) == goal(iota((tall, count), 1)))
+
+    packed_y = half_y(count // 2, lambda at: at // 2)
+    placed_y = half_y(count, lambda at: at // cy * cy + j * (cy // 2) + at % cy // 2)
+    pieces = [part for h in halves for part in parts_of(flat[h], 3)[::-1]]
+    depths = jnp.dot(jnp.concatenate(pieces, axis=0), half_z, preferred_element_type=F32)
     for h in halves:
-        x = sum(jnp.dot(part, half_z, preferred_element_type=F32) for part in parts_of(flat[h], 3)[::-1])
-        x = sum(jnp.dot(half_y, part, preferred_element_type=F32) for part in parts_of(x, 3)[::-1])
+        x = sum(depths[count * n : count * (n + 1)] for n in range(3 * h, 3 * h + 3))
+        rows_y = placed_y if n_gy == 2 and h == 0 else packed_y
+        x = sum(jnp.dot(rows_y, part, preferred_element_type=F32) for part in parts_of(x, 3)[::-1])
         if n_gy == 2:
-            coarse_refs[h][...] = x.reshape(cx // 2, cy, half // 2)
+            coarse_refs[h][...] = x.reshape(cx // 2, -1, half // 2)
         else:
             coarse_refs[0][:, half // 2 * h : half // 2 * (h + 1)] = x
     for copy in out_copies:
@@ -514,8 +519,6 @@
         receiver_cell.reshape(1, sensors),
         trace_offset.reshape(1, sensors),
     )
-    stage_args = sensor_args + fields
-    stage_out = [shape((n_gx, n_gy, 8, 128), F32)] + prep_out
     odd_send = call(
         odd_kernel,
         halo_block,
@@ -524,6 +527,9 @@
         in_specs=[HBM] * 4,
         out_specs=ANY,
     )
+    odd_send, *sensor_args = lax.optimization_barrier((odd_send, *sensor_args))
+    stage_args = (*sensor_args, *fields)
+    stage_out = [shape((n_gx, n_gy, 8, 128), F32)] + prep_out
     packed, *prep = call(
         functools.partial(stage_kernel, n_gx, n_gy, steps, slots, reach),
         stage_out,
@@ -561,7 +567,7 @@
     padded = pltpu.VMEM((3 * cx, 2, rows + 16, nz // 2), F32)
     block = pltpu.VMEM((3 * cx, 2, rows, nz // 2), F32)
     if n_gy == 2:
-        outs = [shape((cx // 2, cy, nz // 4), F32)] * 2
+        outs = [shape((cx // 2, cy, nz // 4), F32), shape((cx // 2, cy // 2, nz // 4), F32)]
     else:
         outs = [shape((cx * cy // 4, nz // 2), F32)]
     buffers = [forward_accel, arrived, odd_got, even_got] + [x for got in side_got for x in (got[2], got[1])]
@@ -580,7 +586,9 @@
     )
     if n_gy == 2:
         final, mine, send = got
-        whole = mine + lax.ppermute(send, "gy", [(0, 1), (1, 0)])
+        got = lax.ppermute(send, "gy", [(0, 1), (1, 0)])
+        own_half = iota(mine.shape, 1) // (cy // 2) == lax.axis_index("gy")
+        whole = jnp.where(own_half, mine, jnp.concatenate([got, got], axis=1))
         sensitivity = jnp.transpose(whole, (0, 2, 1))
     else:
         final, coarse = got

time: 42.3 us -> 42 us (level)
  no operation moved by 1% of the time
where the time goes in v5:
time: 42 us; the launch traced here: 41.8 us
  Pallas kernels  15.8 us (38%)
  starting transfers between devices  14.1 us (34%)
  waiting for transfers between devices  10.4 us (25%)
  between operations  0.76 us (2%)
  other arithmetic  0.72 us (2%)
    pallas_call x3, Pallas kernels, call(): pl.pallas_call(kernel, out_shape=out_shape, in_specs=in_specs or [VMEM] *...  15.8 us
    all_to_all x1, starting transfers between devices, shards(): lax.all_to_all(packed.reshape(n_gx * n_gy, 8, 128), ('gx', 'gy'), split_a...  4.93 us
    ppermute x1, starting transfers between devices, shards(): odd_side = lax.ppermute(prep[2 + 3 * n], ('gx', 'gy'), corner)  4.21 us
    ppermute x1, waiting for transfers between devices, shards(): got = lax.ppermute(send, 'gy', [(0, 1), (1, 0)])  3.47 us
    all_to_all x1, waiting for transfers between devices, shards(): lax.all_to_all(packed.reshape(n_gx * n_gy, 8, 128), ('gx', 'gy'), split_a...  2.82 us
    ppermute x1, starting transfers between devices, shards(): odd_got = lax.ppermute(odd_send, 'gx', odd)  2.75 us
    ppermute x1, waiting for transfers between devices, shards(): odd_side = lax.ppermute(prep[2 + 3 * n], ('gx', 'gy'), corner)  2.66 us
    ppermute x1, waiting for transfers between devices, shards(): even_side = lax.ppermute(prep[3 + 3 * n], ('gx', 'gy'), corner)  1.42 us
  transfers between devices with their start and end apart: 7, of which 4 were waited for; matrix products, arithmetic and copies ran while one was open for 0% of the time, Pallas kernels for 8%

profile of v5, /device:TPU:26, one launch (start us, length us, event | category | flops | bytes accessed | tf_op | source)
XLA Modules:
  0.0 41.8 jit_solution(2298584794453311508)
XLA Ops:
  0.6 2.0 %shard_map.104 = bf16[42,32,256]{2,1,0:T(8,128)(2,1)} custom-call(f32[8,32,256]{2,1,0:T(8,128)} %refs_0_.4, f32[8,32,256]{2,1,0:T(8,128)} %refs_1_.3, f32[8,32,256]{2,1,0:T(8,128)} %refs_2_.3, f32[8,32,256]{2,1,0:T(8,128)} %refs_3_.3), custom_call_target="tpu_custom_call" | custom-call | tf_op jit(solution)/shard_map/pallas_call | solution.py:479
  2.6 2.8 %collective-permute-start = (bf16[42,32,256]{2,1,0:T(8,128)(2,1)}, bf16[42,32,256]{2,1,0:T(8,128)(2,1)S(1)}, u32[]{:S(2)}, u32[]{:S(2)}) collective-permute-start(bf16[42,32,256]{2,1,0:T(8,128)(2,1)} %shard_map.104), channel_id=1, source_target_pairs={{2,4},{6,8},{10,12},{14,16},{18,20},{22,24},{26,28},{4,2},{8,6},{1... | collective-permute-start | bytes 2064392 | tf_op jit(solution)/shard_map/ppermute | solution.py:544
  5.4 0.0 copy-start.1
  5.4 0.0 copy-start.2
  5.4 0.0 copy-start.3
  5.4 3.1 %shard_map.105 = (f32[16,2,8,128]{3,2,1,0:T(8,128)}, bf16[42,32,256]{2,1,0:T(8,128)(2,1)}, f32[4,8,8,256]{3,2,1,0:T(8,128)}, bf16[224,256]{1,0:T(8,128)(2,1)}, bf16[224,256]{1,0:T(8,128)(2,1)}) custom-call(bf16[512,128]{1,0:T(8,128)(2,1)} %refs_0_.3, s32[1,512]{1,0:T(1,128)} %bitcast.9, s32[1,512]{1,0:T(1,128)} %bitcast.10, s32[1,512]{1,0:T(1,128)} %bitcast.11, ...), custom_call_target="tpu_custom_call" | custom-call | tf_op jit(solution)/shard_map/pallas_call | solution.py:479
  8.5 0.0 copy-start
  8.6 0.9 %collective-permute-start.1 = (bf16[42,32,256]{2,1,0:T(8,128)(2,1)}, bf16[42,32,256]{2,1,0:T(8,128)(2,1)S(1)}, u32[]{:S(2)}, u32[]{:S(2)}) collective-permute-start(bf16[42,32,256]{2,1,0:T(8,128)(2,1)} %get-tuple-element.21), channel_id=1, source_target_pairs={{0,2},{2,0},{4,6},{6,4},{8,10},{10,8},{12,14},{14,12},{16,18},{18,... | collective-permute-start | bytes 2064392 | tf_op jit(solution)/shard_map/ppermute | solution.py:559
  9.4 0.5 %collective-permute-start.2 = (f32[4,8,8,256]{3,2,1,0:T(8,128)}, f32[4,8,8,256]{3,2,1,0:T(8,128)S(1)}, u32[]{:S(2)}, u32[]{:S(2)}) collective-permute-start(f32[4,8,8,256]{3,2,1,0:T(8,128)} %get-tuple-element.22), channel_id=1, source_target_pairs={{0,1},{1,0},{2,3},{3,2},{4,5},{5,4},{6,7},{7,6},{8,9},{9,8},{10,11... | collective-permute-start | bytes 786440 | tf_op jit(solution)/shard_map/ppermute | solution.py:554
  9.9 4.9 %all-to-all-start = ((f32[32,8,128]{2,1,0:T(8,128)}), f32[32,8,128]{2,1,0:T(8,128)S(1)}, u32[]{:S(2)}, u32[]{:S(2)}) async-start(f32[32,8,128]{2,1,0:T(8,128)} %bitcast.8), calls=%async_computation | async-start | bytes 262144 | tf_op jit(solution)/shard_map/all_to_all | solution.py:561
  14.9 0.4 collective-permute-start.3
  15.2 4.2 %collective-permute-start.4 = (bf16[224,256]{1,0:T(8,128)(2,1)}, bf16[224,256]{1,0:T(8,128)(2,1)S(1)}, u32[]{:S(2)}, u32[]{:S(2)}) collective-permute-start(bf16[224,256]{1,0:T(8,128)(2,1)} %get-tuple-element.24), channel_id=1, source_target_pairs={{2,5},{3,4},{6,9},{7,8},{10,13},{11,12},{14,17},{15,16},{18,21},{1... | collective-permute-start | bytes 344072 | tf_op jit(solution)/shard_map/ppermute | solution.py:555
  19.5 1.4 %collective-permute-done.3.refs_9_ = bf16[224,256]{1,0:T(8,128)(2,1)S(1)} collective-permute-done((bf16[224,256]{1,0:T(8,128)(2,1)}, bf16[224,256]{1,0:T(8,128)(2,1)S(1)}, u32[]{:S(2)}, u32[]{:S(2)}) %collective-permute-start.3) | collective-permute-done | bytes 114720 | tf_op jit(solution)/shard_map/ppermute | solution.py:557
  20.9 2.7 %collective-permute-done.4.refs_10_ = bf16[224,256]{1,0:T(8,128)(2,1)S(1)} collective-permute-done((bf16[224,256]{1,0:T(8,128)(2,1)}, bf16[224,256]{1,0:T(8,128)(2,1)S(1)}, u32[]{:S(2)}, u32[]{:S(2)}) %collective-permute-start.4) | collective-permute-done | bytes 114720 | tf_op jit(solution)/shard_map/ppermute | solution.py:555
  23.6 2.8 %all-to-all-done = f32[32,8,128]{2,1,0:T(8,128)S(1)} async-done(((f32[32,8,128]{2,1,0:T(8,128)}), f32[32,8,128]{2,1,0:T(8,128)S(1)}, u32[]{:S(2)}, u32[]{:S(2)}) %all-to-all-start) | async-done | bytes 131104 | tf_op jit(solution)/shard_map/all_to_all | solution.py:561
  26.4 0.0 collective-permute-done.2.refs_8_
  26.4 0.0 collective-permute-done.refs_6_
  26.4 0.0 collective-permute-done.1.refs_7_
  26.4 0.0 copy-done.1
  26.4 0.0 copy-done.2
  26.4 0.0 copy-done.3
  26.4 0.0 copy-done
  26.4 10.7 %shard_map.106 = (f32[8,32,256]{2,1,0:T(8,128)}, f32[4,32,64]{2,1,0:T(8,128)S(1)}, f32[4,16,64]{2,1,0:T(8,128)S(1)}) custom-call(f32[8,32,256]{2,1,0:T(8,128)S(1)} %copy-done, f32[8,32,256]{2,1,0:T(8,128)S(1)} %copy-done.1, f32[8,32,256]{2,1,0:T(8,128)S(1)} %copy-done.2, f32[8,32,256]{2,1,0:T(8,128)S(1)} %copy-done.3, bf16[8,8,32,256]{3,2,1,0:T(8,128)(2,1)} %refs_4_.3, ...), custom_call_target="tpu_custom_call" | custom-call | tf_op jit(solution)/shard_map/pallas_call | solution.py:479
  37.1 0.5 %collective-permute-start.5 = (f32[4,16,64]{2,1,0:T(8,128)S(1)}, f32[4,16,64]{2,1,0:T(8,128)S(1)}, u32[]{:S(2)}, u32[]{:S(2)}) collective-permute-start(f32[4,16,64]{2,1,0:T(8,128)S(1)} %get-tuple-element.26), channel_id=1, source_target_pairs={{0,1},{1,0},{2,3},{3,2},{4,5},{5,4},{6,7},{7,6},{8,9},{9,8},{10,11... | collective-permute-start | bytes 49160 | tf_op jit(solution)/shard_map/ppermute | solution.py:589
  37.6 3.5 %collective-permute-done.5 = f32[4,16,64]{2,1,0:T(8,128)S(1)} collective-permute-done((f32[4,16,64]{2,1,0:T(8,128)S(1)}, f32[4,16,64]{2,1,0:T(8,128)S(1)}, u32[]{:S(2)}, u32[]{:S(2)}) %collective-permute-start.5) | collective-permute-done | bytes 16416 | tf_op jit(solution)/shard_map/ppermute | solution.py:589
  41.1 0.7 %fusion = f32[4,64,32]{1,2,0:T(8,128)} fusion(f32[4,32,64]{2,1,0:T(8,128)S(1)} %get-tuple-element.25, f32[4,16,64]{2,1,0:T(8,128)S(1)} %collective-permute-done.5, s32[]{:T(128)S(6)} %axis_index.12, s32[32]{0:T(128)S(1)} %get-tuple-element.28, s32[32]{0:T(128)S(1)} %get-tuple-element.29, pred[32]{0:T(512)(128)(4,1)S(1)} %compare_and_fusion), kind=kLoop, calls=%fused_computation.1 | loop fusion | flops 32768 | bytes 82212 | tf_op jit(solution)/shard_map/transpose | solution.py:592
  (2 shorter events, 0.0 us)
Async XLA Ops:
  2.6 23.8 %collective-permute-start = (bf16[42,32,256]{2,1,0:T(8,128)(2,1)}, bf16[42,32,256]{2,1,0:T(8,128)(2,1)S(1)}, u32[]{:S(2)}, u32[]{:S(2)}) collective-permute-start(bf16[42,32,256]{2,1,0:T(8,128)(2,1)} %shard_map.104), channel_id=1, source_target_pairs={{2,4},{6,8},{10,12},{14,16},{18,20},{22,24},{26,28},{4,2},{8,6},{1... | collective-permute-start | bytes 2064392 | tf_op jit(solution)/shard_map/ppermute | solution.py:544
  5.4 21.0 %copy-start.1 = (f32[8,32,256]{2,1,0:T(8,128)S(1)}, f32[8,32,256]{2,1,0:T(8,128)}, u32[]{:S(2)}) copy-start(f32[8,32,256]{2,1,0:T(8,128)} %refs_1_.3) | copy-start | bytes 786436
  5.4 21.0 %copy-start.2 = (f32[8,32,256]{2,1,0:T(8,128)S(1)}, f32[8,32,256]{2,1,0:T(8,128)}, u32[]{:S(2)}) copy-start(f32[8,32,256]{2,1,0:T(8,128)} %refs_2_.3) | copy-start | bytes 786436
  5.4 21.0 %copy-start.3 = (f32[8,32,256]{2,1,0:T(8,128)S(1)}, f32[8,32,256]{2,1,0:T(8,128)}, u32[]{:S(2)}) copy-start(f32[8,32,256]{2,1,0:T(8,128)} %refs_3_.3) | copy-start | bytes 786436
  8.5 17.9 %copy-start = (f32[8,32,256]{2,1,0:T(8,128)S(1)}, f32[8,32,256]{2,1,0:T(8,128)}, u32[]{:S(2)}) copy-start(f32[8,32,256]{2,1,0:T(8,128)} %refs_0_.4) | copy-start | bytes 786436
  8.6 17.8 %collective-permute-start.1 = (bf16[42,32,256]{2,1,0:T(8,128)(2,1)}, bf16[42,32,256]{2,1,0:T(8,128)(2,1)S(1)}, u32[]{:S(2)}, u32[]{:S(2)}) collective-permute-start(bf16[42,32,256]{2,1,0:T(8,128)(2,1)} %get-tuple-element.21), channel_id=1, source_target_pairs={{0,2},{2,0},{4,6},{6,4},{8,10},{10,8},{12,14},{14,12},{16,18},{18,... | collective-permute-start | bytes 2064392 | tf_op jit(solution)/shard_map/ppermute | solution.py:559
  9.4 17.0 %collective-permute-start.2 = (f32[4,8,8,256]{3,2,1,0:T(8,128)}, f32[4,8,8,256]{3,2,1,0:T(8,128)S(1)}, u32[]{:S(2)}, u32[]{:S(2)}) collective-permute-start(f32[4,8,8,256]{3,2,1,0:T(8,128)} %get-tuple-element.22), channel_id=1, source_target_pairs={{0,1},{1,0},{2,3},{3,2},{4,5},{5,4},{6,7},{7,6},{8,9},{9,8},{10,11... | collective-permute-start | bytes 786440 | tf_op jit(solution)/shard_map/ppermute | solution.py:554
  9.9 16.4 %all-to-all-start = ((f32[32,8,128]{2,1,0:T(8,128)}), f32[32,8,128]{2,1,0:T(8,128)S(1)}, u32[]{:S(2)}, u32[]{:S(2)}) async-start(f32[32,8,128]{2,1,0:T(8,128)} %bitcast.8), calls=%async_computation | async-start | bytes 262144 | tf_op jit(solution)/shard_map/all_to_all | solution.py:561
  14.9 6.0 %collective-permute-start.3 = (bf16[224,256]{1,0:T(8,128)(2,1)}, bf16[224,256]{1,0:T(8,128)(2,1)S(1)}, u32[]{:S(2)}, u32[]{:S(2)}) collective-permute-start(bf16[224,256]{1,0:T(8,128)(2,1)} %get-tuple-element.23), channel_id=1, source_target_pairs={{0,3},{1,2},{2,1},{3,0},{4,7},{5,6},{6,5},{7,4},{8,11},{9,10},{10,... | collective-permute-start | bytes 344072 | tf_op jit(solution)/shard_map/ppermute | solution.py:557
  15.2 8.3 %collective-permute-start.4 = (bf16[224,256]{1,0:T(8,128)(2,1)}, bf16[224,256]{1,0:T(8,128)(2,1)S(1)}, u32[]{:S(2)}, u32[]{:S(2)}) collective-permute-start(bf16[224,256]{1,0:T(8,128)(2,1)} %get-tuple-element.24), channel_id=1, source_target_pairs={{2,5},{3,4},{6,9},{7,8},{10,13},{11,12},{14,17},{15,16},{18,21},{1... | collective-permute-start | bytes 344072 | tf_op jit(solution)/shard_map/ppermute | solution.py:555
  37.1 4.0 %collective-permute-start.5 = (f32[4,16,64]{2,1,0:T(8,128)S(1)}, f32[4,16,64]{2,1,0:T(8,128)S(1)}, u32[]{:S(2)}, u32[]{:S(2)}) collective-permute-start(f32[4,16,64]{2,1,0:T(8,128)S(1)} %get-tuple-element.26), channel_id=1, source_target_pairs={{0,1},{1,0},{2,3},{3,2},{4,5},{5,4},{6,7},{7,6},{8,9},{9,8},{10,11... | collective-permute-start | bytes 49160 | tf_op jit(solution)/shard_map/ppermute | solution.py:589
